TPU v7x, 32 devices: a whole 2x2x4 slice. The times are simulated.
32 devices in a mesh: fsdp: 8 (over y, x, core), sp: 4 (over z).
Axes of the slice: x: 2, y: 2, z: 4, core: 2. Of those that a mesh axis runs over, the one named last changes fastest.
Arguments:
- inputs: bfloat16 [8, 1536, 1024], P('fsdp', 'sp'), may hold values from -6 to 6
- segments: int32 [8, 1536], P('fsdp', 'sp'), may hold values from 0 to 4, as said below
- enc_states: bfloat16 [8, 1024, 1024], P('fsdp', 'sp'), may hold values from -6 to 6
- adapter_pick: int32 [8], P('fsdp'), may hold values from 0 to 7
- qkv_weights: bfloat16 [1, 6, 1024, 1024], P(None, None, 'fsdp'), may hold values from -0.1875 to 0.1875
- out_weights: bfloat16 [1, 2, 1024, 1024], P(None, None, 'fsdp'), may hold values from -0.75 to 0.75
- mlp_in: bfloat16 [1, 1024, 4096], P(None, 'fsdp'), may hold values from -0.1875 to 0.1875
- mlp_out: bfloat16 [1, 4096, 1024], P(None, 'fsdp'), may hold values from -0.09375 to 0.09375
- proj_down: bfloat16 [1, 8, 8, 16, 1024], replicated, may hold values from -0.1875 to 0.1875
- proj_up: bfloat16 [1, 8, 8, 16, 1024], replicated, may hold values from -0.75 to 0.75
- fc1_down: bfloat16 [1, 8, 16, 1024], replicated, may hold values from -0.1875 to 0.1875
- fc1_up: bfloat16 [1, 8, 16, 4096], replicated, may hold values from -0.75 to 0.75
- fc2_down: bfloat16 [1, 8, 16, 4096], replicated, may hold values from -0.09375 to 0.09375
- fc2_up: bfloat16 [1, 8, 16, 1024], replicated, may hold values from -0.75 to 0.75
- cotangent: bfloat16 [8, 1536, 1024], P('fsdp', 'sp'), may hold values from -6 to 6
Outputs:
- output: bfloat16 [8, 1536, 1024], P('fsdp', 'sp')
- input_grad: float32 [8, 1536, 1024], P('fsdp', 'sp')
- memory_grad: float32 [8, 1024, 1024], P('fsdp', 'sp')
- proj_down_grad: float32 [1, 8, 8, 16, 1024], replicated
- proj_up_grad: float32 [1, 8, 8, 16, 1024], replicated
- fc1_down_grad: float32 [1, 8, 16, 1024], replicated
- fc1_up_grad: float32 [1, 8, 16, 4096], replicated
- fc2_down_grad: float32 [1, 8, 16, 4096], replicated
- fc2_up_grad: float32 [1, 8, 16, 1024], replicated
Inputs may be any that keep to these rules, and one draw needn't show every extreme that they name: `segments`: segment numbers never fall along a sequence; segment 2 starts within the first 384 tokens of every sequence and ends within its last 384; the last token is in segment 4.
All inputs are finite; a program needn't handle non-finite values.
Results may differ from a plain program's by a relative error of at most 0.025.
The roundings to bfloat16 on the way count: a program that leaves them out, or rounds other values in their place, can miss the bound.
Values may be sent and summed in bfloat16 or wider, within the bound.
No kernel may reach another device: no remote copies, remote signals or barrier semaphores. Data moves between devices by JAX's collectives and lax.ppermute only.
A program may use at most 192 MiB of HBM per device.

v0:
```python
import jax
import jax.numpy as jnp
from jax import lax
from jax.sharding import PartitionSpec as P

HEAD = 64


norm_eps = 1e-05
masked_fill = -1e30


def matmul(left, right):
    return jnp.dot(left, right, preferred_element_type=jnp.float32)


def project(rows_low, weight, down_proj, up_proj):
    hidden = lax.dot_general(
        rows_low, down_proj, (((1,), (1,)), ((), ())), preferred_element_type=jnp.float32
    ).astype(jnp.bfloat16)
    return (matmul(rows_low, weight) + matmul(hidden, up_proj), hidden)


def project_back(grad_low, rows_low, hidden, weight, down_proj, up_proj):
    contract = (((1,), (1,)), ((), ()))
    across = (((0,), (0,)), ((), ()))
    grad_hidden = lax.dot_general(
        grad_low, up_proj, contract, preferred_element_type=jnp.float32
    ).astype(jnp.bfloat16)
    grad_rows = lax.dot_general(
        grad_low, weight, contract, preferred_element_type=jnp.float32
    ) + matmul(grad_hidden, down_proj)
    grad_up = lax.dot_general(hidden, grad_low, across, preferred_element_type=jnp.float32)
    grad_down = lax.dot_general(grad_hidden, rows_low, across, preferred_element_type=jnp.float32)
    return (grad_rows, grad_down, grad_up)


def project_many(rows_low, weights, downs, ups):
    hidden = jnp.einsum("td,prd->ptr", rows_low, downs, preferred_element_type=jnp.float32).astype(
        jnp.bfloat16
    )
    mixed = jnp.einsum("td,pde->pte", rows_low, weights, preferred_element_type=jnp.float32)
    mixed = mixed + jnp.einsum("ptr,pre->pte", hidden, ups, preferred_element_type=jnp.float32)
    return (mixed.astype(jnp.bfloat16), hidden)


def project_many_back(grads_low, rows_low, hidden, weights, downs, ups):
    grad_hidden = jnp.einsum(
        "pte,pre->ptr", grads_low, ups, preferred_element_type=jnp.float32
    ).astype(jnp.bfloat16)
    grad_rows = jnp.einsum("pte,pde->td", grads_low, weights, preferred_element_type=jnp.float32)
    grad_rows = grad_rows + jnp.einsum(
        "ptr,prd->td", grad_hidden, downs, preferred_element_type=jnp.float32
    )
    grad_up = jnp.einsum("ptr,pte->pre", hidden, grads_low, preferred_element_type=jnp.float32)
    grad_down = jnp.einsum("ptr,td->prd", grad_hidden, rows_low, preferred_element_type=jnp.float32)
    return (grad_rows, grad_down, grad_up)


def normalize(values):
    centered = values - jnp.mean(values, -1, keepdims=True)
    inv_std = lax.rsqrt(jnp.mean(centered * centered, -1, keepdims=True) + norm_eps)
    return (centered * inv_std, inv_std)


def normalize_back(grad_rows, normed, inv_std):
    return inv_std * (
        grad_rows
        - jnp.mean(grad_rows, -1, keepdims=True)
        - normed * jnp.mean(grad_rows * normed, -1, keepdims=True)
    )


def gelu_value(values):
    return 0.5 * values * (1.0 + lax.erf(values * 0.7071067811865476))


def gelu_slope(values):
    return (
        0.5 * (1.0 + lax.erf(values * 0.7071067811865476))
        + values * jnp.exp(-0.5 * values * values) * 0.3989422804014327
    )


def attend(queries, key_rows, value_rows, allowed):
    length, width = queries.shape
    block_rows = min(512, length)
    block_count = length // block_rows
    heads_local = width // HEAD
    keys_h = key_rows.reshape(-1, heads_local, HEAD)
    values_h = value_rows.reshape(-1, heads_local, HEAD)
    scale = HEAD ** (-0.5)

    def one_block(packed):
        block_q, first_row = packed
        scores = (
            jnp.einsum("qhd,khd->hqk", block_q, keys_h, preferred_element_type=jnp.float32) * scale
        )
        if allowed is not None:
            scores = jnp.where(allowed(first_row, block_rows)[None], scores, masked_fill)
        row_max = jnp.max(scores, -1, keepdims=True)
        weights_exp = jnp.exp(scores - row_max)
        row_total = jnp.sum(weights_exp, -1, keepdims=True)
        chances = (weights_exp / row_total).astype(jnp.bfloat16)
        outputs = jnp.einsum("hqk,khd->qhd", chances, values_h, preferred_element_type=jnp.float32)
        return (outputs.astype(jnp.bfloat16), (row_max + jnp.log(row_total))[..., 0])

    starts = jnp.arange(block_count, dtype=jnp.int32) * block_rows
    outputs, log_totals = lax.map(
        one_block, (queries.reshape(block_count, block_rows, heads_local, HEAD), starts)
    )
    return (outputs.reshape(length, width), log_totals)


def attend_back(queries, key_rows, value_rows, log_totals, grad_out, allowed):
    length, width = queries.shape
    block_rows = min(512, length)
    block_count = length // block_rows
    heads_local = width // HEAD
    keys_h = key_rows.reshape(-1, heads_local, HEAD)
    values_h = value_rows.reshape(-1, heads_local, HEAD)
    scale = HEAD ** (-0.5)

    def one_block(totals, packed):
        block_q, first_row, block_lse, block_grad = packed
        scores = (
            jnp.einsum("qhd,khd->hqk", block_q, keys_h, preferred_element_type=jnp.float32) * scale
        )
        if allowed is not None:
            scores = jnp.where(allowed(first_row, block_rows)[None], scores, masked_fill)
        chances = jnp.exp(scores - block_lse[..., None])
        grad_values = totals[1] + jnp.einsum(
            "hqk,qhd->khd",
            chances.astype(jnp.bfloat16),
            block_grad,
            preferred_element_type=jnp.float32,
        )
        grad_chances = jnp.einsum(
            "qhd,khd->hqk", block_grad, values_h, preferred_element_type=jnp.float32
        )
        grad_scores = (
            chances * (grad_chances - jnp.sum(grad_chances * chances, -1, keepdims=True))
        ).astype(jnp.bfloat16)
        grad_q = (
            jnp.einsum("hqk,khd->qhd", grad_scores, keys_h, preferred_element_type=jnp.float32)
            * scale
        )
        grad_keys = (
            totals[0]
            + jnp.einsum("hqk,qhd->khd", grad_scores, block_q, preferred_element_type=jnp.float32)
            * scale
        )
        return ((grad_keys, grad_values), grad_q)

    starts = jnp.arange(block_count, dtype=jnp.int32) * block_rows
    empty = jnp.zeros(keys_h.shape, jnp.float32)
    sliced_q = queries.reshape(block_count, block_rows, heads_local, HEAD)
    sliced_grad = grad_out.reshape(block_count, block_rows, heads_local, HEAD)
    totals, grad_q = lax.scan(
        one_block, (empty, empty), (sliced_q, starts, log_totals, sliced_grad)
    )
    return (
        grad_q.reshape(length, width),
        totals[0].reshape(-1, width),
        totals[1].reshape(-1, width),
    )


def shards(
    inputs,
    segments,
    enc_states,
    adapter_pick,
    qkv_weights,
    out_weights,
    mlp_in,
    mlp_out,
    proj_down,
    proj_up,
    fc1_down,
    fc1_up,
    fc2_down,
    fc2_up,
    cotangent,
):
    stream = inputs[0].astype(jnp.float32)
    memory = enc_states[0]
    seg_full = lax.all_gather(segments, "sp", axis=1, tiled=True)[0]
    length = seg_full.shape[0]
    positions = jnp.arange(length, dtype=jnp.int32)
    picked = (adapter_pick[0] == jnp.arange(proj_down.shape[2], dtype=jnp.int32)).astype(
        jnp.bfloat16
    )
    adapt_down = jnp.einsum(
        "a,lpard->lprd", picked, proj_down, preferred_element_type=jnp.float32
    ).astype(jnp.bfloat16)
    adapt_up = jnp.einsum(
        "a,lpard->lprd", picked, proj_up, preferred_element_type=jnp.float32
    ).astype(jnp.bfloat16)
    first_down = jnp.einsum(
        "a,lard->lrd", picked, fc1_down, preferred_element_type=jnp.float32
    ).astype(jnp.bfloat16)
    first_up = jnp.einsum("a,lard->lrd", picked, fc1_up, preferred_element_type=jnp.float32).astype(
        jnp.bfloat16
    )
    second_down = jnp.einsum(
        "a,lard->lrd", picked, fc2_down, preferred_element_type=jnp.float32
    ).astype(jnp.bfloat16)
    second_up = jnp.einsum(
        "a,lard->lrd", picked, fc2_up, preferred_element_type=jnp.float32
    ).astype(jnp.bfloat16)

    def causal_segments(first_row, block_rows):
        query_seg = lax.dynamic_slice_in_dim(seg_full, first_row, block_rows)
        query_pos = first_row + jnp.arange(block_rows, dtype=jnp.int32)
        return (query_seg[:, None] == seg_full[None, :]) & (
            positions[None, :] <= query_pos[:, None]
        )

    def to_tokens(heads_rows):
        return lax.all_to_all(heads_rows, "sp", split_axis=0, concat_axis=1, tiled=True)

    def grad_to_heads(token_rows):
        return lax.all_to_all(token_rows, "sp", split_axis=1, concat_axis=0, tiled=True)

    layers = qkv_weights.shape[0]
    layer_at = 0
    frozen = (
        lax.all_gather(qkv_weights[layer_at], "fsdp", axis=1, tiled=True),
        lax.all_gather(out_weights[layer_at], "fsdp", axis=1, tiled=True),
        lax.all_gather(mlp_in[layer_at], "fsdp", axis=0, tiled=True),
        lax.all_gather(mlp_out[layer_at], "fsdp", axis=0, tiled=True),
    )
    w_in, w_out, w_up, w_down = frozen
    stream_low = stream.astype(jnp.bfloat16)
    qkv_low, hidden_qkv = project_many(
        stream_low, w_in[0:3], adapt_down[layer_at, 0:3], adapt_up[layer_at, 0:3]
    )
    mem_low, hidden_mem = project_many(
        memory, w_in[4:6], adapt_down[layer_at, 4:6], adapt_up[layer_at, 4:6]
    )
    heads_qkv = lax.all_to_all(qkv_low, "sp", split_axis=2, concat_axis=1, tiled=True)
    heads_mem = lax.all_to_all(mem_low, "sp", split_axis=2, concat_axis=1, tiled=True)
    self_out, self_lse = attend(heads_qkv[0], heads_qkv[1], heads_qkv[2], causal_segments)
    self_tok = to_tokens(self_out)
    branch, hidden_so = project(self_tok, w_out[0], adapt_down[layer_at, 6], adapt_up[layer_at, 6])
    first_norm, first_std = normalize(stream + branch)
    first_low = first_norm.astype(jnp.bfloat16)
    cross_q, hidden_cq = project(first_low, w_in[3], adapt_down[layer_at, 3], adapt_up[layer_at, 3])
    heads_cq = lax.all_to_all(
        cross_q.astype(jnp.bfloat16), "sp", split_axis=1, concat_axis=0, tiled=True
    )
    cross_out, cross_lse = attend(heads_cq, heads_mem[0], heads_mem[1], None)
    cross_tok = to_tokens(cross_out)
    branch, hidden_co = project(cross_tok, w_out[1], adapt_down[layer_at, 7], adapt_up[layer_at, 7])
    second_norm, second_std = normalize(first_norm + branch)
    second_low = second_norm.astype(jnp.bfloat16)
    hidden_pre, hidden_fc1 = project(second_low, w_up, first_down[layer_at], first_up[layer_at])
    gelu_low = gelu_value(hidden_pre).astype(jnp.bfloat16)
    branch, hidden_fc2 = project(gelu_low, w_down, second_down[layer_at], second_up[layer_at])
    third_norm, third_std = normalize(second_norm + branch)
    saved = [
        (
            frozen,
            stream_low,
            hidden_qkv,
            hidden_mem,
            heads_qkv,
            heads_mem,
            self_lse,
            self_tok,
            hidden_so,
            first_norm,
            first_std,
            first_low,
            hidden_cq,
            heads_cq,
            cross_lse,
            cross_tok,
            hidden_co,
            second_norm,
            second_std,
            second_low,
            hidden_pre,
            hidden_fc1,
            gelu_low,
            hidden_fc2,
            third_norm,
            third_std,
        )
    ]
    stream = third_norm
    grad_stream = cotangent[0].astype(jnp.float32)
    grad_memory = jnp.zeros(memory.shape, jnp.float32)
    collected = []
    for layer_at in reversed(range(layers)):
        (
            frozen,
            stream_low,
            hidden_qkv,
            hidden_mem,
            heads_qkv,
            heads_mem,
            self_lse,
            self_tok,
            hidden_so,
            first_norm,
            first_std,
            first_low,
            hidden_cq,
            heads_cq,
            cross_lse,
            cross_tok,
            hidden_co,
            second_norm,
            second_std,
            second_low,
            hidden_pre,
            hidden_fc1,
            gelu_low,
            hidden_fc2,
            third_norm,
            third_std,
        ) = saved[layer_at]
        frozen = (
            lax.all_gather(qkv_weights[layer_at], "fsdp", axis=1, tiled=True),
            lax.all_gather(out_weights[layer_at], "fsdp", axis=1, tiled=True),
            lax.all_gather(mlp_in[layer_at], "fsdp", axis=0, tiled=True),
            lax.all_gather(mlp_out[layer_at], "fsdp", axis=0, tiled=True),
        )
        w_in, w_out, w_up, w_down = frozen
        grad_third = normalize_back(grad_stream, third_norm, third_std)
        back_fc2 = project_back(
            grad_third.astype(jnp.bfloat16),
            gelu_low,
            hidden_fc2,
            w_down,
            second_down[layer_at],
            second_up[layer_at],
        )
        grad_pre = (back_fc2[0] * gelu_slope(hidden_pre)).astype(jnp.bfloat16)
        back_fc1 = project_back(
            grad_pre, second_low, hidden_fc1, w_up, first_down[layer_at], first_up[layer_at]
        )
        grad_second = normalize_back(grad_third + back_fc1[0], second_norm, second_std)
        back_co = project_back(
            grad_second.astype(jnp.bfloat16),
            cross_tok,
            hidden_co,
            w_out[1],
            adapt_down[layer_at, 7],
            adapt_up[layer_at, 7],
        )
        grad_cross_heads = grad_to_heads(back_co[0].astype(jnp.bfloat16))
        grad_cq, grad_ck, grad_cv = attend_back(
            heads_cq, heads_mem[0], heads_mem[1], cross_lse, grad_cross_heads, None
        )
        grad_cq_tok = lax.all_to_all(
            grad_cq.astype(jnp.bfloat16), "sp", split_axis=0, concat_axis=1, tiled=True
        )
        back_cq = project_back(
            grad_cq_tok,
            first_low,
            hidden_cq,
            w_in[3],
            adapt_down[layer_at, 3],
            adapt_up[layer_at, 3],
        )
        grad_first = normalize_back(grad_second + back_cq[0], first_norm, first_std)
        back_so = project_back(
            grad_first.astype(jnp.bfloat16),
            self_tok,
            hidden_so,
            w_out[0],
            adapt_down[layer_at, 6],
            adapt_up[layer_at, 6],
        )
        grad_self_heads = grad_to_heads(back_so[0].astype(jnp.bfloat16))
        grad_q, grad_k, grad_v = attend_back(
            heads_qkv[0], heads_qkv[1], heads_qkv[2], self_lse, grad_self_heads, causal_segments
        )
        grad_qkv, grad_mem = (
            lax.all_to_all(
                jnp.stack([grad_q, grad_k, grad_v]).astype(jnp.bfloat16),
                "sp",
                split_axis=1,
                concat_axis=2,
                tiled=True,
            ),
            lax.all_to_all(
                jnp.stack([grad_ck, grad_cv]).astype(jnp.bfloat16),
                "sp",
                split_axis=1,
                concat_axis=2,
                tiled=True,
            ),
        )
        back_qkv = project_many_back(
            grad_qkv,
            stream_low,
            hidden_qkv,
            w_in[0:3],
            adapt_down[layer_at, 0:3],
            adapt_up[layer_at, 0:3],
        )
        back_mem = project_many_back(
            grad_mem,
            memory,
            hidden_mem,
            w_in[4:6],
            adapt_down[layer_at, 4:6],
            adapt_up[layer_at, 4:6],
        )
        grad_memory = back_mem[0]
        grad_stream = grad_first + back_qkv[0]
        layer_down = jnp.concatenate(
            [back_qkv[1], back_cq[1][None], back_mem[1], back_so[1][None], back_co[1][None]], axis=0
        )
        layer_up = jnp.concatenate(
            [back_qkv[2], back_cq[2][None], back_mem[2], back_so[2][None], back_co[2][None]], axis=0
        )
        collected.insert(
            0, (layer_down, layer_up, back_fc1[1], back_fc1[2], back_fc2[1], back_fc2[2])
        )
    selected = tuple((jnp.stack([entry[slot] for entry in collected]) for slot in range(6)))
    picked_wide = picked.astype(jnp.float32)
    wide_proj = picked_wide[None, None, :, None, None]
    wide_fc = picked_wide[None, :, None, None]
    totals = lax.psum(
        (
            selected[0][:, :, None] * wide_proj,
            selected[1][:, :, None] * wide_proj,
            selected[2][:, None] * wide_fc,
            selected[3][:, None] * wide_fc,
            selected[4][:, None] * wide_fc,
            selected[5][:, None] * wide_fc,
        ),
        ("fsdp", "sp"),
    )
    return (
        stream.astype(jnp.bfloat16)[None],
        grad_stream[None],
        grad_memory[None],
        totals[0],
        totals[1],
        totals[2],
        totals[3],
        totals[4],
        totals[5],
    )


def solution(mesh):
    return jax.shard_map(
        shards,
        mesh=mesh,
        in_specs=(
            P("fsdp", "sp", None),
            P("fsdp", "sp"),
            P("fsdp", "sp", None),
            P("fsdp"),
            P(None, None, "fsdp", None),
            P(None, None, "fsdp", None),
            P(None, "fsdp", None),
            P(None, "fsdp", None),
            P(),
            P(),
            P(),
            P(),
            P(),
            P(),
            P("fsdp", "sp", None),
        ),
        out_specs=(
            P("fsdp", "sp", None),
            P("fsdp", "sp", None),
            P("fsdp", "sp", None),
            P(),
            P(),
            P(),
            P(),
            P(),
            P(),
        ),
        check_vma=False,
    )
```

profile of v0, /device:TPU:0, one launch (start us, length us, event | category | flops | bytes accessed | tf_op | source)
XLA Modules:
  0.0 1062.0 jit_solution(16498625020738035902)
XLA Ops:
  17.9 69.8 %all-gather.9.cloned.1.call-done = bf16[1,6,1024,1024]{2,3,1,0:T(8,128)(2,1)} async-done(((bf16[1,6,128,1024]{2,3,1,0:T(8,128)(2,1)}), bf16[1,6,1024,1024]{2,3,1,0:T(8,128)(2,1)}) %all-gather.9.cloned.1.call-update) | async-done | bytes 12582928 | tf_op jit(solution)/shard_map/all_gather | solution.py:229
  87.7 7.6 fusion.99
  104.6 75.8 %all_gather.19 = s32[1,1536]{1,0:T(1,128)S(1)} all-gather(s32[1,384]{1,0:T(1,128)S(1)} %copy-done.99), channel_id=1, replica_groups=mesh['fsdp'=8,'sp'=4] {'sp'}, dimensions={1}, use_global_device_ids=true | all-gather | bytes 7680 | tf_op jit(solution)/shard_map/all_gather | solution.py:188
  189.6 49.0 %while.56 = (s32[]{:T(128)}, bf16[3,512,4,64]{1,3,2,0:T(8,128)(2,1)}, f32[3,4,512]{2,1,0:T(4,128)S(1)}, s32[3]{0:T(128)S(1)}, s32[1536]{0:T(1024)S(1)}, /*index=...) while((s32[]{:T(128)}, ...), condition=%wide.region_3.4_spmd.clone, body=%wide.region_0.3_spmd.clone.sunk | while | flops 845543936 | bytes 43087028 | solution.py:109
  255.9 11.6 %all-to-all-done.1 = bf16[4,384,256]{1,2,0:T(8,128)(2,1)S(1)} async-done(((bf16[4,384,256]{1,2,0:T(8,128)(2,1)}), bf16[4,384,256]{1,2,0:T(8,128)(2,1)S(1)}, u32[]{:S(2)}, u32[]{:S(2)}) %all-to-all-start.1) | async-done | bytes 786464 | tf_op jit(solution)/shard_map/all_to_all | solution.py:221
  281.6 14.5 %all-to-all-done.3 = bf16[2,256,1024]{1,0,2:T(2,128)(2,1)S(1)} async-done(((bf16[2,256,1024]{1,0,2:T(2,128)(2,1)}), bf16[2,256,1024]{1,0,2:T(2,128)(2,1)S(1)}, u32[]{:S(2)}, u32[]{:S(2)}) %all-to-all-start.3) | async-done | bytes 1048608 | tf_op jit(solution)/shard_map/all_to_all | solution.py:243
  304.1 16.0 %all-to-all-done.2 = bf16[384,4,256]{0,2,1:T(8,128)(2,1)} async-done(((bf16[384,4,256]{0,2,1:T(8,128)(2,1)}), bf16[384,4,256]{0,2,1:T(8,128)(2,1)}, u32[]{:S(2)}, u32[]{:S(2)}) %all-to-all-start.2) | async-done | bytes 786464 | tf_op jit(solution)/shard_map/all_to_all | solution.py:250
  322.7 16.1 %while.55 = (s32[]{:T(128)}, bf16[3,512,4,64]{1,3,2,0:T(8,128)(2,1)S(1)}, f32[3,4,512]{2,1,0:T(4,128)S(1)}, bf16[3,512,4,64]{1,3,2,0:T(8,128)(2,1)S(1)}, bf16[10...) while((s32[]{:T(128)}, bf16[3,512,4,64]{1,3,2,0:T(8,128)(2,1)S(1)}, ...), condition=%wide.region_9.10_spmd, body=%wide.region_6.9_spmd.sunk | while | flops 555874304 | bytes 26804312 | solution.py:109
  357.5 12.1 %all-to-all-done.4 = bf16[4,384,256]{1,2,0:T(8,128)(2,1)S(1)} async-done(((bf16[4,384,256]{1,2,0:T(8,128)(2,1)}), bf16[4,384,256]{1,2,0:T(8,128)(2,1)S(1)}, u32[]{:S(2)}, u32[]{:S(2)}) %all-to-all-start.4) | async-done | bytes 786464 | tf_op jit(solution)/shard_map/all_to_all | solution.py:221
  375.6 5.8 fusion.89
  388.1 6.8 fusion.85
  398.2 12.0 %fusion.83 = f32[384,4096]{1,0:T(8,128)} fusion(bf16[1,4096,1024]{2,1,0:T(8,128)(2,1)} %all-gather.15.cloned.1.call-done, f32[384,1024]{1,0:T(8,128)S(1)} %get-tuple-element.515), kind=kOutput, calls=%fused_computation.97 | convolution fusion | flops 3221618688 | bytes 16252928 | tf_op jit(solution)/shard_map/dot_general | solution.py:30
  430.6 19.6 %all-to-all-done.5 = bf16[384,4,256]{0,2,1:T(8,128)(2,1)} async-done(((bf16[384,4,256]{0,2,1:T(8,128)(2,1)}), bf16[384,4,256]{0,2,1:T(8,128)(2,1)}, u32[]{:S(2)}, u32[]{:S(2)}) %all-to-all-start.5) | async-done | bytes 786464 | tf_op jit(solution)/shard_map/all_to_all | solution.py:224
  459.6 63.7 %while.57 = (s32[]{:T(128)}, f32[1024,4,64]{0,2,1:T(8,128)S(1)}, f32[1024,4,64]{0,2,1:T(8,128)S(1)}, bf16[3,512,4,64]{1,3,2,0:T(8,128)(2,1)}, bf16[3,512,4,64]{1...) while((s32[]{:T(128)}, f32[1024,4,64]{0,2,1:T(8,128)S(1)}, ...), condition=%wide.region_20.21_spmd.clone, body=%wide.region_18.20_spmd.clone.sunk | while | flops 1368782848 | bytes 143714576 | solution.py:159
  530.8 22.3 %all_to_all.168 = bf16[4,384,256]{1,2,0:T(8,128)(2,1)S(1)} all-to-all(bf16[4,384,256]{1,2,0:T(8,128)(2,1)S(1)} %copy.111), channel_id=1, replica_groups=mesh['fsdp'=8,'sp'=4] {'sp'}, dimensions={0} | all-to-all | bytes 1572864 | tf_op jit(solution)/shard_map/all_to_all | solution.py:358
  571.2 16.9 %all-to-all-done.7 = bf16[384,4,256]{0,2,1:T(8,128)(2,1)} async-done(((bf16[384,4,256]{0,2,1:T(8,128)(2,1)}), bf16[384,4,256]{0,2,1:T(8,128)(2,1)}, u32[]{:S(2)}, u32[]{:S(2)}) %all-to-all-start.7) | async-done | bytes 786464 | tf_op jit(solution)/shard_map/all_to_all | solution.py:224
  598.1 100.4 %while.58 = (s32[]{:T(128)}, f32[1536,4,64]{0,2,1:T(8,128)}, f32[1536,4,64]{0,2,1:T(8,128)}, bf16[3,512,4,64]{1,3,2,0:T(8,128)(2,1)}, bf16[3,512,4,64]{1,3,2,0:T...) while((s32[]{:T(128)}, f32[1536,4,64]{0,2,1:T(8,128)}, ...), condition=%wide.region_25.26_spmd.clone, body=%wide.region_23.25_spmd.clone.sunk | while | flops 2046032384 | bytes 206903088 | solution.py:159
  621.6 6.2 fusion.330
  648.5 5.8 fusion.328
  654.3 6.2 fusion.330
  688.4 6.2 fusion.330
  725.0 61.2 %all-to-all-done.8 = bf16[3,1536,256]{2,0,1:T(4,128)(2,1)} async-done(((bf16[3,1536,256]{2,0,1:T(4,128)(2,1)}), bf16[3,1536,256]{2,0,1:T(4,128)(2,1)}, u32[]{:S(2)}, u32[]{:S(2)}) %all-to-all-start.8) | async-done | bytes 2359328 | tf_op jit(solution)/shard_map/all_to_all | solution.py:383
  804.4 6.6 fusion.119
  811.0 231.8 %all-reduce.3.cloned.1.call-done = (f32[1,8,8,16,1024]{4,3,2,1,0:T(8,128)}, f32[1,8,8,16,1024]{4,3,2,1,0:T(8,128)}, f32[1,8,16,1024]{3,2,1,0:T(8,128)}, f32[1,8,...) async-done(((f32[1,8,8,16,1024]{4,3,2,1,0:T(8,128)}, f32[1,8,8,16,1024]{4,3,2,1,0:T(8,128)}, f32[1,8,16,1024]{3,2,1,0:T(8,128)}, ...) | async-done | bytes 13631504 | tf_op jit(solution)/shard_map/psum | solution.py:429
  (505 shorter events, 418.4 us)
Async XLA Ops:
  7.2 80.6 %all-gather.9.cloned.1.call-start = ((), (), s32[]{:S(2)}) async-start(), calls=%async_computation.10 | async-start | bytes 14155776 | tf_op jit(solution)/shard_map/all_gather | solution.py:229
  10.0 262.7 %all-gather.11.cloned.1.call-start = ((), (), s32[]{:S(2)}) async-start(), calls=%async_computation.11 | async-start | bytes 4718592 | tf_op jit(solution)/shard_map/all_gather | solution.py:230
  13.1 356.5 %copy-start.53 = (bf16[1,8,16,1024]{3,2,1,0:T(8,128)(2,1)}, bf16[1,8,16,1024]{3,2,1,0:T(8,128)(2,1)S(1)}, u32[]{:S(2)}) copy-start(bf16[1,8,16,1024]{3,2,1,0:T(8,128)(2,1)S(1)} %copy.186) | copy-start | bytes 786436
  14.6 543.4 %copy-start.51 = (bf16[1,8,16,1024]{3,2,1,0:T(8,128)(2,1)}, bf16[1,8,16,1024]{3,2,1,0:T(8,128)(2,1)S(1)}, u32[]{:S(2)}) copy-start(bf16[1,8,16,1024]{3,2,1,0:T(8,128)(2,1)S(1)} %copy.187) | copy-start | bytes 786436
  99.1 81.4 %all-to-all-start = ((bf16[3,384,1024]{1,0,2:T(4,128)(2,1)}), bf16[3,384,1024]{1,0,2:T(4,128)(2,1)}, u32[]{:S(2)}, u32[]{:S(2)}) async-start(bf16[3,384,1024]{1,0,2:T(4,128)(2,1)} %copy.92), calls=%async_computation | async-start | bytes 6291456 | tf_op jit(solution)/shard_map/all_to_all | solution.py:242
  103.9 271.8 %all-gather.13.cloned.1.call-start = ((), (), s32[]{:S(2)}) async-start(), calls=%async_computation.12 | async-start | bytes 9437184 | tf_op jit(solution)/shard_map/all_gather | solution.py:231
  245.4 22.0 %all-to-all-start.1 = ((bf16[4,384,256]{1,2,0:T(8,128)(2,1)}), bf16[4,384,256]{1,2,0:T(8,128)(2,1)S(1)}, u32[]{:S(2)}, u32[]{:S(2)}) async-start(bf16[4,384,256]{1,2,0:T(8,128)(2,1)} %copy.96), calls=%async_computation.1 | async-start | bytes 1572864 | tf_op jit(solution)/shard_map/all_to_all | solution.py:221
  248.9 139.2 %all-gather.15.cloned.1.call-start = ((), (), s32[]{:S(2)}) async-start(), calls=%async_computation.13 | async-start | bytes 9437184 | tf_op jit(solution)/shard_map/all_gather | solution.py:232
  267.4 28.7 %all-to-all-start.3 = ((bf16[2,256,1024]{1,0,2:T(2,128)(2,1)}), bf16[2,256,1024]{1,0,2:T(2,128)(2,1)S(1)}, u32[]{:S(2)}, u32[]{:S(2)}) async-start(bf16[2,256,1024]{1,0,2:T(2,128)(2,1)} %copy.100), calls=%async_computation.3 | async-start | bytes 2097152 | tf_op jit(solution)/shard_map/all_to_all | solution.py:243
  276.3 94.6 %copy-start.93 = (f32[384]{0:T(512)}, f32[384]{0:T(512)S(1)}, u32[]{:S(2)}) copy-start(f32[384]{0:T(512)S(1)} %broadcast_multiply_fusion.14) | copy-start | bytes 4612
  276.6 94.3 %copy-start.95 = (f32[384]{0:T(512)}, f32[384]{0:T(512)S(1)}, u32[]{:S(2)}) copy-start(f32[384]{0:T(512)S(1)} %add_rsqrt_fusion.2) | copy-start | bytes 4612
  296.1 24.0 %all-to-all-start.2 = ((bf16[384,4,256]{0,2,1:T(8,128)(2,1)}), bf16[384,4,256]{0,2,1:T(8,128)(2,1)}, u32[]{:S(2)}, u32[]{:S(2)}) async-start(bf16[384,4,256]{0,2,1:T(8,128)(2,1)} %bitcast.32), calls=%async_computation.2 | async-start | bytes 1572864 | tf_op jit(solution)/shard_map/all_to_all | solution.py:250
  346.3 23.3 %all-to-all-start.4 = ((bf16[4,384,256]{1,2,0:T(8,128)(2,1)}), bf16[4,384,256]{1,2,0:T(8,128)(2,1)S(1)}, u32[]{:S(2)}, u32[]{:S(2)}) async-start(bf16[4,384,256]{1,2,0:T(8,128)(2,1)} %copy.105), calls=%async_computation.4 | async-start | bytes 1572864 | tf_op jit(solution)/shard_map/all_to_all | solution.py:221
  397.9 22.3 %copy-start.19 = (f32[384,1024]{1,0:T(8,128)}, f32[384,1024]{1,0:T(8,128)S(1)}, u32[]{:S(2)}) copy-start(f32[384,1024]{1,0:T(8,128)S(1)} %get-tuple-element.515) | copy-start | bytes 4718596
  397.9 18.7 %slice-start.2 = ((s8[8388608]{0:T(1024)(128)(4,1)}), s8[4194304]{0:T(1024)(128)(4,1)S(1)}, s32[]{:S(2)}) async-start(s8[8388608]{0:T(1024)(128)(4,1)} %bitcast.577), calls=%async_computation.17 | async-start | bytes 8388608
  426.2 24.0 %all-to-all-start.5 = ((bf16[384,4,256]{0,2,1:T(8,128)(2,1)}), bf16[384,4,256]{0,2,1:T(8,128)(2,1)}, u32[]{:S(2)}, u32[]{:S(2)}) async-start(bf16[384,4,256]{0,2,1:T(8,128)(2,1)} %bitcast.65), calls=%async_computation.5 | async-start | bytes 1572864 | tf_op jit(solution)/shard_map/all_to_all | solution.py:224
  530.8 23.8 %copy-start.10 = (f32[384,1024]{1,0:T(8,128)S(1)}, f32[384,1024]{1,0:T(8,128)}, u32[]{:S(2)}) copy-start(f32[384,1024]{1,0:T(8,128)} %copy-done.9) | copy-start | bytes 4718596
  530.8 23.8 %copy-start.13 = (f32[384,1024]{1,0:T(8,128)S(1)}, f32[384,1024]{1,0:T(8,128)}, u32[]{:S(2)}) copy-start(f32[384,1024]{1,0:T(8,128)} %copy-done.12) | copy-start | bytes 4718596
  530.8 23.8 %copy-start.94 = (f32[384]{0:T(512)S(1)}, f32[384]{0:T(512)}, u32[]{:S(2)}) copy-start(f32[384]{0:T(512)} %copy-done.93) | copy-start | bytes 4612
  530.8 23.8 %copy-start.96 = (f32[384]{0:T(512)S(1)}, f32[384]{0:T(512)}, u32[]{:S(2)}) copy-start(f32[384]{0:T(512)} %copy-done.95) | copy-start | bytes 4612
  564.7 23.4 %all-to-all-start.7 = ((bf16[384,4,256]{0,2,1:T(8,128)(2,1)}), bf16[384,4,256]{0,2,1:T(8,128)(2,1)}, u32[]{:S(2)}, u32[]{:S(2)}) async-start(bf16[384,4,256]{0,2,1:T(8,128)(2,1)} %bitcast.567), calls=%async_computation.7 | async-start | bytes 1572864 | tf_op jit(solution)/shard_map/all_to_all | solution.py:224
  588.1 123.0 %all-to-all-start.9 = ((bf16[2,1024,256]{2,0,1:T(2,128)(2,1)}), bf16[2,1024,256]{2,0,1:T(2,128)(2,1)}, u32[]{:S(2)}, u32[]{:S(2)}) async-start(bf16[2,1024,256]{2,0,1:T(2,128)(2,1)} %copy.121), calls=%async_computation.9 | async-start | bytes 2097152 | tf_op jit(solution)/shard_map/all_to_all | solution.py:390
  711.2 75.0 %all-to-all-start.8 = ((bf16[3,1536,256]{2,0,1:T(4,128)(2,1)}), bf16[3,1536,256]{2,0,1:T(4,128)(2,1)}, u32[]{:S(2)}, u32[]{:S(2)}) async-start(bf16[3,1536,256]{2,0,1:T(4,128)(2,1)} %copy.117), calls=%async_computation.8 | async-start | bytes 6291456 | tf_op jit(solution)/shard_map/all_to_all | solution.py:383
  716.4 326.4 %all-reduce.3.cloned.1.call-start = ((), (), s32[]{:S(2)}) async-start(), calls=%async_computation.14 | async-start | bytes 27262976 | tf_op jit(solution)/shard_map/psum | solution.py:429
  (108 other events, 449.9 us)
Sparse Core Ops, SparseCore 0:
  10.5 77.2 all-gather.8
  89.6 36.7 all-gather.10
  128.3 54.3 all-gather.12
  251.3 54.8 all-gather.14
  798.3 244.5 all-reduce.2
where the time goes:
time: 1070 us; the launch traced here: 1060 us
  waiting for transfers between devices  455 us (43%)
  matrix products  258 us (24%)
  local copies, waits for them, and re-layouts  120 us (11%)
  blocking collectives  98.1 us (9%)
  other arithmetic  63 us (6%)
  starting transfers between devices  39 us (4%)
  between operations  16.4 us (2%)
  loops' own time  12.2 us (1%)
    psum x1, waiting for transfers between devices, shards(): lax.psum((selected[0][:, :, None] * wide_proj, selected[1][:, :, None] *...  232 us
    all_gather x1, blocking collectives, shards(): seg_full = lax.all_gather(segments, 'sp', axis=1, tiled=True)[0]  75.8 us
    all_gather x1, waiting for transfers between devices, shards(): lax.all_gather(qkv_weights[layer_at], 'fsdp', axis=1, tiled=True)  69.8 us
    all_to_all x1, waiting for transfers between devices, shards(): lax.all_to_all(jnp.stack([grad_q, grad_k, grad_v]).astype(jnp.bfloat16),...  61.2 us
    dot_general x15, matrix products, matmul(): return jnp.dot(left, right, preferred_element_type=jnp.float32)  40 us
    all_to_all x2, waiting for transfers between devices, grad_to_heads(): lax.all_to_all(token_rows, 'sp', split_axis=1, concat_axis=0, tiled=True)  36.6 us
    dot_general x12, matrix products, one_block(): jnp.einsum('qhd,khd->hqk', block_q, keys_h, preferred_element_type=jnp.fl...  34.7 us
    dot_general x6, matrix products, one_block(): jnp.einsum('hqk,khd->qhd', grad_scores, keys_h, preferred_element_type=jn...  31 us
  transfers between devices with their start and end apart: 14, of which 9 were waited for; matrix products, arithmetic and copies ran while one was open for 25% of the time, Pallas kernels for 0%

commit v1 on v0

v1 whole, which is shorter than its diff:
```python
import functools

import jax
import jax.numpy as jnp
from jax import lax
from jax.experimental import pallas as pl
from jax.experimental.pallas import tpu as pltpu
from jax.sharding import Mesh
from jax.sharding import PartitionSpec as P

HEAD = 64
PAIR = 2 * HEAD
LANES = 128
NORM_EPS = 1e-05
FAR = -1e30
SEG_KINDS = 5
SEG_LANE = 3
F32 = jnp.float32
BF16 = jnp.bfloat16
VMEM = 60 * 1024 * 1024


def dot(left, right, dims):
    return lax.dot_general(left, right, ((dims[0], dims[1]), ((), ())), preferred_element_type=F32)


def nn(left, right):
    return dot(left, right, ((1,), (0,)))


def nt(left, right):
    return dot(left, right, ((1,), (1,)))


def tn(left, right):
    return dot(left, right, ((0,), (0,)))


def lane_of(rows):
    return lax.broadcasted_iota(jnp.int32, (rows, LANES), 1)


def split_pair(rows):
    low = lane_of(rows.shape[0]) < HEAD
    zero = jnp.zeros_like(rows)
    return jnp.concatenate([jnp.where(low, rows, zero), jnp.where(low, zero, rows)], axis=0)


def join_pair(rows):
    half = rows.shape[0] // 2
    return jnp.where(lane_of(half) < HEAD, rows[:half], rows[half:])


def three_terms(column):
    high = column.astype(BF16)
    rest = column - high.astype(F32)
    mid = rest.astype(BF16)
    low = (rest - mid.astype(F32)).astype(BF16)
    return high, mid, low


def spread_terms(terms, rest):
    lane = lane_of(terms[0].shape[0])
    out = rest
    for at, term in enumerate(terms):
        out = jnp.where(lane == at, term, out)
    return out


def attend_kernel(blocks, block, causal, s_ref, q_ref, qaug_ref, k_ref, v_ref, kaug_ref, out_ref, aug_ref, m_ref, l_ref, acc_ref):
    rows = q_ref.shape[0]
    q = q_ref[...] * jnp.asarray(HEAD**-0.5, BF16)
    qaug = qaug_ref[...]
    qaug2 = jnp.concatenate([qaug, qaug], axis=0)
    qa = jnp.concatenate([split_pair(q), qaug2], axis=1)

    def scores_of(at):
        keys = jnp.concatenate([k_ref[at * block : (at + 1) * block], kaug_ref[at * block : (at + 1) * block]], axis=1)
        return nt(qa, keys)

    scores = scores_of(0)
    if causal:
        row = lax.broadcasted_iota(jnp.int32, (rows, block), 0)
        col = lax.broadcasted_iota(jnp.int32, (rows, block), 1)
        keep = col <= row
        scores = jnp.where(jnp.concatenate([keep, keep], axis=0), scores, FAR)
    top = jnp.max(scores, axis=1, keepdims=True)
    weights = jnp.exp(scores - top)
    m_ref[...] = top
    l_ref[...] = jnp.sum(weights, axis=1, keepdims=True)
    acc_ref[...] = nn(weights.astype(BF16), v_ref[0:block])

    def more(at):
        scores = scores_of(at)
        old = m_ref[...]
        top = jnp.maximum(old, jnp.max(scores, axis=1, keepdims=True))
        scale = jnp.exp(old - top)
        weights = jnp.exp(scores - top)
        m_ref[...] = top
        l_ref[...] = l_ref[...] * scale + jnp.sum(weights, axis=1, keepdims=True)
        acc_ref[...] = acc_ref[...] * scale + nn(weights.astype(BF16), v_ref[at * block : (at + 1) * block])

    for at in range(1, blocks):
        if causal:
            pl.when(s_ref[0] >= at)(functools.partial(more, at))
        else:
            more(at)
    total = l_ref[...]
    out_ref[...] = join_pair(acc_ref[...] / total).astype(BF16)
    lse = m_ref[...] + jnp.log(total)
    aug_ref[0] = spread_terms(three_terms(-lse), qaug2)


def attend(place, queries, qaug, keys, values, kaug, block, causal):
    rows, width = queries.shape
    total = keys.shape[0]
    pairs = width // PAIR
    kernel = functools.partial(attend_kernel, total // block, block, causal)
    return pl.pallas_call(
        kernel,
        grid_spec=pltpu.PrefetchScalarGridSpec(
            num_scalar_prefetch=1,
            grid=(pairs,),
            in_specs=[
                pl.BlockSpec((rows, PAIR), lambda h, s: (0, h)),
                pl.BlockSpec((rows, LANES), lambda h, s: (0, 0)),
                pl.BlockSpec((total, PAIR), lambda h, s: (0, h)),
                pl.BlockSpec((total, PAIR), lambda h, s: (0, h)),
                pl.BlockSpec((total, LANES), lambda h, s: (0, 0)),
            ],
            out_specs=[
                pl.BlockSpec((rows, PAIR), lambda h, s: (0, h)),
                pl.BlockSpec((1, 2 * rows, LANES), lambda h, s: (h, 0, 0)),
            ],
            scratch_shapes=[
                pltpu.VMEM((2 * rows, 1), F32),
                pltpu.VMEM((2 * rows, 1), F32),
                pltpu.VMEM((2 * rows, PAIR), F32),
            ],
        ),
        out_shape=[
            jax.ShapeDtypeStruct((rows, width), BF16),
            jax.ShapeDtypeStruct((pairs, 2 * rows, LANES), BF16),
        ],
        compiler_params=pltpu.CompilerParams(vmem_limit_bytes=VMEM),
        cost_estimate=pl.CostEstimate(flops=4 * rows * total * width, bytes_accessed=4 * total * width, transcendentals=rows * total * width // HEAD),
    )(place, queries, qaug, keys, values, kaug)


def attend_back_kernel(blocks, block, causal, s_ref, q_ref, aug_ref, k_ref, v_ref, kaug_ref, do_ref, o_ref, dq_ref, dk_ref, dv_ref, acc_ref):
    rows = q_ref.shape[0]
    q = split_pair(q_ref[...] * jnp.asarray(HEAD**-0.5, BF16))
    grads = do_ref[...]
    dot_rows = grads.astype(F32) * o_ref[...].astype(F32)
    low = lane_of(rows) < HEAD
    delta = jnp.concatenate(
        [
            jnp.sum(jnp.where(low, dot_rows, 0.0), axis=1, keepdims=True),
            jnp.sum(jnp.where(low, 0.0, dot_rows), axis=1, keepdims=True),
        ],
        axis=0,
    )
    grads = split_pair(grads)
    qa = jnp.concatenate([q, aug_ref[0]], axis=1)
    ga = jnp.concatenate([grads, spread_terms(three_terms(-delta), jnp.zeros((2 * rows, LANES), BF16))], axis=1)

    def one(at, first):
        span = slice(at * block, (at + 1) * block)
        kaug = kaug_ref[span]
        keys = k_ref[span]
        scores = nt(jnp.concatenate([keys, kaug], axis=1), qa)
        if causal and first:
            row = lax.broadcasted_iota(jnp.int32, (block, rows), 0)
            col = lax.broadcasted_iota(jnp.int32, (block, rows), 1)
            keep = row <= col
            scores = jnp.where(jnp.concatenate([keep, keep], axis=1), scores, FAR)
        chances = jnp.exp(scores)
        slopes = nt(jnp.concatenate([v_ref[span], kaug], axis=1), ga)
        low_slopes = (chances * slopes).astype(BF16)
        dv_ref[span] = nn(chances.astype(BF16), grads).astype(BF16)
        dk_ref[span] = nn(low_slopes, q).astype(BF16)
        part = tn(low_slopes, keys)
        if first:
            acc_ref[...] = part
        else:
            acc_ref[...] += part

    def none(at):
        span = slice(at * block, (at + 1) * block)
        dv_ref[span] = jnp.zeros((block, PAIR), BF16)
        dk_ref[span] = jnp.zeros((block, PAIR), BF16)

    one(0, True)
    for at in range(1, blocks):
        if causal:
            pl.when(s_ref[0] >= at)(functools.partial(one, at, False))
            pl.when(s_ref[0] < at)(functools.partial(none, at))
        else:
            one(at, False)
    dq_ref[...] = (join_pair(acc_ref[...]) * HEAD**-0.5).astype(BF16)


def attend_back(place, queries, aug, keys, values, kaug, grads, outs, block, causal):
    rows, width = queries.shape
    total = keys.shape[0]
    pairs = width // PAIR
    kernel = functools.partial(attend_back_kernel, total // block, block, causal)
    by_head = pl.BlockSpec((rows, PAIR), lambda h, s: (0, h))
    keys_by_head = pl.BlockSpec((total, PAIR), lambda h, s: (0, h))
    return pl.pallas_call(
        kernel,
        grid_spec=pltpu.PrefetchScalarGridSpec(
            num_scalar_prefetch=1,
            grid=(pairs,),
            in_specs=[
                by_head,
                pl.BlockSpec((1, 2 * rows, LANES), lambda h, s: (h, 0, 0)),
                keys_by_head,
                keys_by_head,
                pl.BlockSpec((total, LANES), lambda h, s: (0, 0)),
                by_head,
                by_head,
            ],
            out_specs=[by_head, keys_by_head, keys_by_head],
            scratch_shapes=[pltpu.VMEM((2 * rows, PAIR), F32)],
        ),
        out_shape=[
            jax.ShapeDtypeStruct((rows, width), BF16),
            jax.ShapeDtypeStruct((total, width), BF16),
            jax.ShapeDtypeStruct((total, width), BF16),
        ],
        compiler_params=pltpu.CompilerParams(vmem_limit_bytes=VMEM),
        cost_estimate=pl.CostEstimate(flops=10 * rows * total * width, bytes_accessed=8 * total * width, transcendentals=rows * total * width // HEAD),
    )(place, queries, aug, keys, values, kaug, grads, outs)


def project(rows_low, weight, down, up):
    hidden = nt(rows_low, down).astype(BF16)
    return nn(rows_low, weight) + nn(hidden, up), hidden


def project_back(grad_low, rows_low, hidden, weight, down, up):
    grad_hidden = nt(grad_low, up).astype(BF16)
    grad_rows = nt(grad_low, weight) + nn(grad_hidden, down)
    return grad_rows, tn(grad_hidden, rows_low), tn(hidden, grad_low)


def normalize(values):
    centered = values - jnp.mean(values, -1, keepdims=True)
    inv_std = lax.rsqrt(jnp.mean(centered * centered, -1, keepdims=True) + NORM_EPS)
    return centered * inv_std, inv_std


def normalize_back(grads, normed, inv_std):
    return inv_std * (grads - jnp.mean(grads, -1, keepdims=True) - normed * jnp.mean(grads * normed, -1, keepdims=True))


def gelu_value(values):
    return 0.5 * values * (1.0 + lax.erf(values * 0.7071067811865476))


def gelu_slope(values):
    return 0.5 * (1.0 + lax.erf(values * 0.7071067811865476)) + values * jnp.exp(-0.5 * values * values) * 0.3989422804014327


def make_shards(mesh):
    chips, cores, span = mesh.shape["chip"], mesh.shape["core"], mesh.shape["sp"]
    plane = ("chip", "core")

    def up(values):
        return lax.ppermute(values, "sp", [(i, i + 1) for i in range(span - 1)])

    def down(values):
        return lax.ppermute(values, "sp", [(i + 1, i) for i in range(span - 1)])

    def turn(values, by):
        return lax.ppermute(values, "sp", [(i, (i + by) % span) for i in range(span)])

    def gather_plane(values):
        return lax.all_gather(values, plane, axis=0, tiled=True)

    def shards(
        inputs,
        segments,
        enc_states,
        adapter_pick,
        qkv_weights,
        out_weights,
        mlp_in,
        mlp_out,
        proj_down,
        proj_up,
        fc1_down,
        fc1_up,
        fc2_down,
        fc2_up,
        cotangent,
    ):
        x_low = inputs[0]
        mem_own = enc_states[0]
        seg_own = segments[0]
        pick = adapter_pick[0]
        place = lax.axis_index("sp").astype(jnp.int32)[None]
        tokens, width = x_low.shape
        rank = proj_down.shape[3]

        blocks, seg_blocks, mems = [x_low], [seg_own], [mem_own]
        for _ in range(1, span):
            blocks.append(up(blocks[-1]))
            seg_blocks.append(up(seg_blocks[-1]))
        for by in range(1, span):
            mems.append(turn(mem_own, by))
        x_all = jnp.concatenate(blocks, axis=0)
        seg_all = jnp.concatenate(seg_blocks, axis=0)
        mem_all = jnp.concatenate(mems, axis=0)

        lane = jnp.arange(LANES, dtype=jnp.int32)[None, :]
        in_seg = (lane >= SEG_LANE) & (lane < SEG_LANE + SEG_KINDS)
        q_aug = jnp.where(in_seg & (lane - SEG_LANE == seg_own[:, None]), 1.0, 0.0).astype(BF16)
        k_aug = jnp.where(lane < SEG_LANE, 1.0, jnp.where(in_seg & (lane - SEG_LANE != seg_all[:, None]), FAR, 0.0)).astype(BF16)
        q_aug_free = jnp.zeros((tokens, LANES), BF16)
        k_aug_free = jnp.broadcast_to(jnp.where(lane < SEG_LANE, 1.0, 0.0), (mem_all.shape[0], LANES)).astype(BF16)

        a_proj = lax.dynamic_index_in_dim(proj_down[0], pick, 1, False)
        b_proj = lax.dynamic_index_in_dim(proj_up[0], pick, 1, False)
        a_fc1 = lax.dynamic_index_in_dim(fc1_down[0], pick, 0, False)
        b_fc1 = lax.dynamic_index_in_dim(fc1_up[0], pick, 0, False)
        a_fc2 = lax.dynamic_index_in_dim(fc2_down[0], pick, 0, False)
        b_fc2 = lax.dynamic_index_in_dim(fc2_up[0], pick, 0, False)

        w_self = [gather_plane(qkv_weights[0, p]) for p in range(6)]
        w_out = [gather_plane(out_weights[0, p]) for p in range(2)]
        w_up = gather_plane(mlp_in[0])
        w_down = gather_plane(mlp_out[0])

        q, r_q = project(x_low, w_self[0], a_proj[0], b_proj[0])
        k, r_k = project(x_all, w_self[1], a_proj[1], b_proj[1])
        v, r_v = project(x_all, w_self[2], a_proj[2], b_proj[2])
        q, k, v = q.astype(BF16), k.astype(BF16), v.astype(BF16)
        o, aug = attend(place, q, q_aug, k, v, k_aug, tokens, True)
        branch, r_so = project(o, w_out[0], a_proj[6], b_proj[6])
        h1, std1 = normalize(x_low.astype(F32) + branch)
        h1_low = h1.astype(BF16)
        kc, r_kc = project(mem_all, w_self[4], a_proj[4], b_proj[4])
        vc, r_vc = project(mem_all, w_self[5], a_proj[5], b_proj[5])
        kc, vc = kc.astype(BF16), vc.astype(BF16)
        qc, r_cq = project(h1_low, w_self[3], a_proj[3], b_proj[3])
        qc = qc.astype(BF16)
        mem_block = min(512, mem_all.shape[0])
        oc, aug_c = attend(place, qc, q_aug_free, kc, vc, k_aug_free, mem_block, False)
        branch, r_co = project(oc, w_out[1], a_proj[7], b_proj[7])
        h2, std2 = normalize(h1 + branch)
        h2_low = h2.astype(BF16)
        pre, r_fc1 = project(h2_low, w_up, a_fc1, b_fc1)
        g = gelu_value(pre).astype(BF16)
        branch, r_fc2 = project(g, w_down, a_fc2, b_fc2)
        y, std3 = normalize(h2 + branch)

        d3 = normalize_back(cotangent[0].astype(F32), y, std3)
        dg, da_fc2, db_fc2 = project_back(d3.astype(BF16), g, r_fc2, w_down, a_fc2, b_fc2)
        dpre = (dg * gelu_slope(pre)).astype(BF16)
        dh2, da_fc1, db_fc1 = project_back(dpre, h2_low, r_fc1, w_up, a_fc1, b_fc1)
        d2 = normalize_back(d3 + dh2, h2, std2)
        doc, da_co, db_co = project_back(d2.astype(BF16), oc, r_co, w_out[1], a_proj[7], b_proj[7])
        dqc, dkc, dvc = attend_back(place, qc, aug_c, kc, vc, k_aug_free, doc.astype(BF16), oc, mem_block, False)
        dh1, da_cq, db_cq = project_back(dqc, h1_low, r_cq, w_self[3], a_proj[3], b_proj[3])
        dmem_k, da_kc, db_kc = project_back(dkc, mem_all, r_kc, w_self[4], a_proj[4], b_proj[4])
        dmem_v, da_vc, db_vc = project_back(dvc, mem_all, r_vc, w_self[5], a_proj[5], b_proj[5])
        dmem_parts = (dmem_k + dmem_v).reshape(span, -1, width)
        dmem = dmem_parts[0]
        for by in range(1, span):
            dmem = dmem + turn(dmem_parts[by].astype(BF16), -by).astype(F32)
        d1 = normalize_back(d2 + dh1, h1, std1)
        do, da_so, db_so = project_back(d1.astype(BF16), o, r_so, w_out[0], a_proj[6], b_proj[6])
        dq, dk, dv = attend_back(place, q, aug, k, v, k_aug, do.astype(BF16), o, tokens, True)
        dx_q, da_q, db_q = project_back(dq, x_low, r_q, w_self[0], a_proj[0], b_proj[0])
        dx_k, da_k, db_k = project_back(dk, x_all, r_k, w_self[1], a_proj[1], b_proj[1])
        dx_v, da_v, db_v = project_back(dv, x_all, r_v, w_self[2], a_proj[2], b_proj[2])
        dx_parts = (dx_k + dx_v).reshape(span, tokens, width)
        dx = dx_parts[span - 1]
        for at in reversed(range(span - 1)):
            dx = dx_parts[at] + down(dx.astype(BF16)).astype(F32)
        dx = d1 + dx_q + dx

        def everywhere(parts):
            sizes = [p.size // width for p in parts]
            flat = jnp.concatenate([p.reshape(-1, width) for p in parts], axis=0)
            flat = lax.psum(flat.astype(BF16), "sp")
            return lax.all_gather(flat, plane, axis=0, tiled=False), sizes

        picks = lax.all_gather(adapter_pick, plane, axis=0, tiled=True)
        mlp_parts = (da_fc1, db_fc1, da_fc2, db_fc2)
        proj_parts = [da_q, da_k, da_v, da_cq, da_kc, da_vc, da_so, da_co, db_q, db_k, db_v, db_cq, db_kc, db_vc, db_so, db_co]
        flat, sizes = everywhere(list(mlp_parts) + proj_parts)
        hot = (picks[None, :] == jnp.arange(proj_down.shape[2], dtype=jnp.int32)[:, None]).astype(F32)
        wide = jnp.sum(hot[:, :, None, None] * flat.astype(F32)[None], axis=1)
        outs, at = [], 0
        for size, like in zip(sizes[:4], (fc1_down, fc1_up, fc2_down, fc2_up)):
            outs.append(wide[:, at : at + size].reshape(like.shape))
            at += size
        kinds = 8 * rank
        total_down = wide[:, at : at + kinds].reshape(-1, 8, rank, width).transpose(1, 0, 2, 3)[None]
        total_up = wide[:, at + kinds : at + 2 * kinds].reshape(-1, 8, rank, width).transpose(1, 0, 2, 3)[None]
        return (y.astype(BF16)[None], dx[None], dmem[None], total_down, total_up, *outs)

    return shards


def solution(mesh):
    count = mesh.shape["fsdp"]
    fine = Mesh(mesh.devices.reshape(count // 2, 2, mesh.shape["sp"]), ("chip", "core", "sp"))
    fsdp = ("chip", "core")
    row = P(fsdp, "sp", None)
    return jax.shard_map(
        make_shards(fine),
        mesh=fine,
        in_specs=(
            row,
            P(fsdp, "sp"),
            row,
            P(fsdp),
            P(None, None, fsdp, None),
            P(None, None, fsdp, None),
            P(None, fsdp, None),
            P(None, fsdp, None),
            P(),
            P(),
            P(),
            P(),
            P(),
            P(),
            row,
        ),
        out_specs=(row, row, row, P(), P(), P(), P(), P(), P()),
        check_vma=False,
    )
```

time: 1070 us -> 744 us (0.70)
  waiting for transfers between devices: 455 us -> 296 us
  blocking collectives: 98.1 us -> 8.17 us
  Pallas kernels: 0 us -> 75.5 us
  local copies, waits for them, and re-layouts: 120 us -> 44.6 us
  matrix products: 258 us -> 199 us
  other arithmetic: 63 us -> 37.5 us
  starting transfers between devices: 39 us -> 52.2 us
  loops' own time: 12.2 us -> 0 us
    psum x1, waiting for transfers between devices: 232 us -> 67.6 us  [everywhere(): flat = lax.psum(flat.astype(BF16), 'sp')]
    all_to_all x9 -> x0, waiting for transfers between devices: 152 us -> none  [the longest x1 61.2 us: shards(): lax.all_to_all(jnp.stack([grad_q, grad_k, grad_v]).astype(jnp.bfloat16),...]
    ppermute x0 -> x15, waiting for transfers between devices: none -> 121 us  [the longest x6 54.6 us: up(): return lax.ppermute(values, 'sp', [(i, i + 1) for i in range(span - 1)])]
    all_gather x1 -> x0, blocking collectives: 75.8 us -> none  [shards(): seg_full = lax.all_gather(segments, 'sp', axis=1, tiled=True)[0]]
    pallas_call x0 -> x4, Pallas kernels: none -> 75.5 us  [the longest x2 38.2 us: attend_back(): pl.pallas_call(kernel, grid_spec=pltpu.PrefetchScalarGridSpec(num_scalar_...]
    dot_general x104 -> x80, matrix products: 258 us -> 199 us  [dot(): lax.dot_general(left, right, ((dims[0], dims[1]), ((), ())), preferred_el...]
    ppermute x0 -> x15, starting transfers between devices: none -> 51.7 us  [the longest x6 34.8 us: up(): return lax.ppermute(values, 'sp', [(i, i + 1) for i in range(span - 1)])]
    all_to_all x9 -> x0, starting transfers between devices: 38.2 us -> none  [the longest x2 8.58 us: grad_to_heads(): lax.all_to_all(token_rows, 'sp', split_axis=1, concat_axis=0, tiled=True)]
  transfers between devices with their start and end apart: 14 -> 27, of which waited for: 9 -> 12; matrix products, arithmetic and copies ran while one was open for 25% -> 18% of each run, Pallas kernels for 0% -> 5%
where the time goes in v1:
time: 744 us; the launch traced here: 730 us
  waiting for transfers between devices  296 us (40%)
  matrix products  199 us (27%)
  Pallas kernels  75.5 us (10%)
  starting transfers between devices  52.2 us (7%)
  local copies, waits for them, and re-layouts  44.6 us (6%)
  other arithmetic  37.5 us (5%)
  between operations  15.8 us (2%)
  blocking collectives  8.17 us (1%)
    dot_general x80, matrix products, dot(): lax.dot_general(left, right, ((dims[0], dims[1]), ((), ())), preferred_el...  199 us
    all_gather x10, waiting for transfers between devices, gather_plane(): return lax.all_gather(values, plane, axis=0, tiled=True)  103 us
    psum x1, waiting for transfers between devices, everywhere(): flat = lax.psum(flat.astype(BF16), 'sp')  67.6 us
    ppermute x6, waiting for transfers between devices, up(): return lax.ppermute(values, 'sp', [(i, i + 1) for i in range(span - 1)])  54.6 us
    ppermute x3, waiting for transfers between devices, down(): return lax.ppermute(values, 'sp', [(i + 1, i) for i in range(span - 1)])  47.4 us
    pallas_call x2, Pallas kernels, attend_back(): pl.pallas_call(kernel, grid_spec=pltpu.PrefetchScalarGridSpec(num_scalar_...  38.2 us
    pallas_call x2, Pallas kernels, attend(): pl.pallas_call(kernel, grid_spec=pltpu.PrefetchScalarGridSpec(num_scalar_...  37.4 us
    ppermute x6, starting transfers between devices, up(): return lax.ppermute(values, 'sp', [(i, i + 1) for i in range(span - 1)])  34.8 us
  transfers between devices with their start and end apart: 27, of which 12 were waited for; matrix products, arithmetic and copies ran while one was open for 18% of the time, Pallas kernels for 5%

profile of v1, /device:TPU:0, one launch (start us, length us, event | category | flops | bytes accessed | tf_op | source)
XLA Modules:
  0.0 729.6 jit_solution(12437622906143654067)
XLA Ops:
  34.6 37.3 %collective-permute-done.3 = s32[384]{0:T(512)S(1)} collective-permute-done((s32[384]{0:T(512)S(1)}, s32[384]{0:T(512)S(1)}, u32[]{:S(2)}, u32[]{:S(2)}) %collective-permute-start.3) | collective-permute-done | bytes 1568 | tf_op jit(solution)/shard_map/ppermute | solution.py:271
  71.9 13.9 %collective-permute-start.4 = (s32[384]{0:T(512)S(1)}, s32[384]{0:T(512)S(1)}, u32[]{:S(2)}, u32[]{:S(2)}) collective-permute-start(s32[384]{0:T(512)S(1)} %collective-permute-done.3), channel_id=1, source_target_pairs={{0,1},{1,2},{2,3},{4,5},{5,6},{6,7},{8,9},{9,10},{10,11},{12,13},{... | collective-permute-start | bytes 4616 | tf_op jit(solution)/shard_map/ppermute | solution.py:271
  99.8 11.4 %collective-permute-done.1 = bf16[384,1024]{1,0:T(8,128)(2,1)} collective-permute-done((bf16[384,1024]{1,0:T(8,128)(2,1)}, bf16[384,1024]{1,0:T(8,128)(2,1)}, u32[]{:S(2)}, u32[]{:S(2)}) %collective-permute-start.1) | collective-permute-done | bytes 786464 | tf_op jit(solution)/shard_map/ppermute | solution.py:271
  147.2 9.4 %add_convert_fusion.1.k_ref = bf16[1536,1024]{1,0:T(8,128)(2,1)} fusion(f32[1536,1024]{1,0:T(8,128)} %fusion.115, bf16[1536,1024]{1,0:T(8,128)(2,1)} %copy-done.1, bf16[1,1,1024,1024]{3,2,1,0:T(8,128)(2,1)} %all-gather.26.cloned.1.call-done), kind=kOutput, calls=%fused_computation.20 | convolution fusion | flops 3224371200 | bytes 14680064 | tf_op jit(solution)/shard_map/dot_general | solution.py:24
  156.7 9.6 %add_convert_fusion.v_ref = bf16[1536,1024]{1,0:T(8,128)(2,1)} fusion(f32[1536,1024]{1,0:T(8,128)} %fusion.116, bf16[1536,1024]{1,0:T(8,128)(2,1)} %copy-done.1, bf16[1,1,1024,1024]{3,2,1,0:T(8,128)(2,1)} %all-gather.28.cloned.1.call-done), kind=kOutput, calls=%fused_computation.19 | convolution fusion | flops 3224371200 | bytes 14680064 | tf_op jit(solution)/shard_map/dot_general | solution.py:24
  166.3 11.1 %shard_map.214 = (bf16[384,1024]{1,0:T(8,128)(2,1)}, bf16[8,768,128]{2,1,0:T(8,128)(2,1)}) custom-call(s32[1]{0:T(128)} %bitcast.1.s_ref, bf16[384,1024]{1,0:T(8,128)(2,1)} %add_convert_fusion.7.q_ref, bf16[384,128]{1,0:T(8,128)(2,1)} %select_convert_fusion.1.qaug_ref, bf16[1536,1024]{1,0:T(8,128)(2,1)} %add_convert_fusion.1.k_ref, ...), custom_call_target="tpu_custom_call" | custom-call | flops 2415919104 | bytes 6291456 | tf_op jit(solution)/shard_map/pallas_call | solution.py:119
  193.2 7.1 add_convert_fusion.3.k_ref
  200.3 21.7 %all-gather.36.cloned.1.call-done = bf16[1,1,1024,1024]{3,2,1,0:T(8,128)(2,1)} async-done(((bf16[1,1,128,1024]{3,2,1,0:T(8,128)(2,1)}), bf16[1,1,1024,1024]{3,2,1,0:T(8,128)(2,1)}) %all-gather.36.cloned.1.call-update) | async-done | bytes 2097168 | tf_op jit(solution)/shard_map/all_gather | solution.py:280
  222.1 7.1 add_convert_fusion.2.v_ref
  230.6 26.3 %shard_map.215 = (bf16[384,1024]{1,0:T(8,128)(2,1)}, bf16[8,768,128]{2,1,0:T(8,128)(2,1)}) custom-call(s32[1]{0:T(128)} %bitcast.1.s_ref, bf16[384,1024]{1,0:T(8,128)(2,1)} %add_convert_fusion.6.q_ref, bf16[384,128]{1,0:T(8,128)(2,1)} %broadcast_in_dim.89.qaug_ref, bf16[1024,1024]{1,0:T(8,128)(2,1)} %add_convert_fusion.3.k_ref, ...), custom_call_target="tpu_custom_call" | custom-call | flops 1610612736 | bytes 4194304 | tf_op jit(solution)/shard_map/pallas_call | solution.py:119
  268.6 39.6 %all-gather.40.cloned.1.call-done = bf16[1,1024,4096]{2,1,0:T(8,128)(2,1)} async-done(((bf16[1,128,4096]{2,1,0:T(8,128)(2,1)}), bf16[1,1024,4096]{2,1,0:T(8,128)(2,1)}) %all-gather.40.cloned.1.call-update) | async-done | bytes 8388624 | tf_op jit(solution)/shard_map/all_gather | solution.py:280
  322.6 41.8 %all-gather.42.cloned.1.call-done = bf16[1,4096,1024]{2,1,0:T(8,128)(2,1)} async-done(((bf16[1,512,1024]{2,1,0:T(8,128)(2,1)}), bf16[1,4096,1024]{2,1,0:T(8,128)(2,1)}) %all-gather.42.cloned.1.call-update) | async-done | bytes 8388624 | tf_op jit(solution)/shard_map/all_gather | solution.py:280
  364.4 6.9 fusion.2
  376.0 11.8 %fusion = f32[384,4096]{1,0:T(8,128)} fusion(bf16[1,4096,1024]{2,1,0:T(8,128)(2,1)} %all-gather.42.cloned.1.call-done, f32[384,1024]{1,0:T(8,128)S(1)} %get-tuple-element.42), kind=kOutput, calls=%fused_computation.2 | convolution fusion | flops 3221618688 | bytes 16252928 | tf_op jit(solution)/shard_map/dot_general | solution.py:24
  409.0 24.1 %shard_map.216 = (bf16[384,1024]{1,0:T(8,128)(2,1)}, bf16[1024,1024]{1,0:T(8,128)(2,1)}, bf16[1024,1024]{1,0:T(8,128)(2,1)}) custom-call(s32[1]{0:T(128)} %bitcast.1.s_ref, bf16[384,1024]{1,0:T(8,128)(2,1)} %add_convert_fusion.6.q_ref, bf16[8,768,128]{2,1,0:T(8,128)(2,1)} %get-tuple-element.21.aug_ref, bf16[1024,1024]{1,0:T(8,128)(2,1)} %add_convert_fusion.3.k_ref, ...), custom_call_target="tpu_custom_call" | custom-call | flops 4026531840 | bytes 8388608 | tf_op jit(solution)/shard_map/pallas_call | solution.py:210
  442.6 14.1 %shard_map.217 = (bf16[384,1024]{1,0:T(8,128)(2,1)}, bf16[1536,1024]{1,0:T(8,128)(2,1)}, bf16[1536,1024]{1,0:T(8,128)(2,1)}) custom-call(s32[1]{0:T(128)} %bitcast.1.s_ref, bf16[384,1024]{1,0:T(8,128)(2,1)} %add_convert_fusion.7.q_ref, bf16[8,768,128]{2,1,0:T(8,128)(2,1)} %get-tuple-element.23.aug_ref, bf16[1536,1024]{1,0:T(8,128)(2,1)} %add_convert_fusion.1.k_ref, ...), custom_call_target="tpu_custom_call" | custom-call | flops 6039797760 | bytes 12582912 | tf_op jit(solution)/shard_map/pallas_call | solution.py:210
  491.6 67.6 %all-reduce.3.cloned.1.call-done = bf16[1,416,1024]{2,1,0:T(8,128)(2,1)} async-done(((bf16[1,416,1024]{2,1,0:T(8,128)(2,1)}), bf16[1,416,1024]{2,1,0:T(8,128)(2,1)}) %all-reduce.3.cloned.1.call-update) | async-done | bytes 851984 | tf_op jit(solution)/shard_map/psum | solution.py:388
  560.7 8.2 %all-reduce = s32[8]{0:T(128)S(1)} all-reduce(s32[8]{0:T(128)S(1)} %dynamic-update-slice), channel_id=1, replica_groups=mesh['chip'=4,'core'=2,'sp'=4] {'chip','core'}, use_global_device_ids=true, to_apply=%add | all-reduce | flops 8 | bytes 64
  590.8 9.0 %collective-permute-done.9 = bf16[384,1024]{1,0:T(8,128)(2,1)S(1)} collective-permute-done((bf16[384,1024]{1,0:T(8,128)(2,1)S(1)}, bf16[384,1024]{1,0:T(8,128)(2,1)S(1)}, u32[]{:S(2)}, u32[]{:S(2)}) %collective-permute-start.9) | collective-permute-done | bytes 786464 | tf_op jit(solution)/shard_map/ppermute | solution.py:274
  608.8 26.8 %collective-permute-done.10 = bf16[384,1024]{1,0:T(8,128)(2,1)S(1)} collective-permute-done((bf16[384,1024]{1,0:T(8,128)(2,1)S(1)}, bf16[384,1024]{1,0:T(8,128)(2,1)S(1)}, u32[]{:S(2)}, u32[]{:S(2)}) %collective-permute-start.10) | collective-permute-done | bytes 786464 | tf_op jit(solution)/shard_map/ppermute | solution.py:274
  637.7 19.1 %collective-permute-done.13 = bf16[256,1024]{1,0:T(8,128)(2,1)S(1)} collective-permute-done((bf16[256,1024]{1,0:T(8,128)(2,1)S(1)}, bf16[256,1024]{1,0:T(8,128)(2,1)S(1)}, u32[]{:S(2)}, u32[]{:S(2)}) %collective-permute-start.13) | collective-permute-done | bytes 524320 | tf_op jit(solution)/shard_map/ppermute | solution.py:277
  658.1 11.6 %collective-permute-done.11 = bf16[384,1024]{1,0:T(8,128)(2,1)S(1)} collective-permute-done((bf16[384,1024]{1,0:T(8,128)(2,1)S(1)}, bf16[384,1024]{1,0:T(8,128)(2,1)S(1)}, u32[]{:S(2)}, u32[]{:S(2)}) %collective-permute-start.11) | collective-permute-done | bytes 786464 | tf_op jit(solution)/shard_map/ppermute | solution.py:274
  672.2 9.5 %convert_element_type.219 = f32[8,416,1024]{2,1,0:T(8,128)} convert(bf16[8,416,1024]{2,1,0:T(8,128)(2,1)} %all-gather.22.cloned.1.call-done) | non-fusion elementwise | flops 3407872 | bytes 20447232 | tf_op jit(solution)/shard_map/convert_element_type | solution.py:396
  681.7 18.5 %multiply_reduce_fusion = f32[8,416,1024]{2,1,0:T(8,128)} fusion(f32[8,416,1024]{2,1,0:T(8,128)} %convert_element_type.219, f32[8,8]{1,0:T(8,128)S(1)} %fusion.166), kind=kLoop, calls=%fused_computation | loop fusion | flops 51118080 | bytes 27263232 | tf_op jit(solution)/shard_map/reduce_sum | solution.py:396
  (301 shorter events, 250.4 us)
Async XLA Ops:
  7.2 135.9 %all-gather.24.cloned.1.call-start = ((), (), s32[]{:S(2)}) async-start(), calls=%async_computation.2 | async-start | bytes 2359296 | tf_op jit(solution)/shard_map/all_gather | solution.py:280
  10.0 137.3 %all-gather.26.cloned.1.call-start = ((), (), s32[]{:S(2)}) async-start(), calls=%async_computation.3 | async-start | bytes 2359296 | tf_op jit(solution)/shard_map/all_gather | solution.py:280
  10.7 146.0 %all-gather.28.cloned.1.call-start = ((), (), s32[]{:S(2)}) async-start(), calls=%async_computation.4 | async-start | bytes 2359296 | tf_op jit(solution)/shard_map/all_gather | solution.py:280
  11.5 169.6 %all-gather.30.cloned.1.call-start = ((), (), s32[]{:S(2)}) async-start(), calls=%async_computation.5 | async-start | bytes 2359296 | tf_op jit(solution)/shard_map/all_gather | solution.py:280
  12.4 176.6 %all-gather.32.cloned.1.call-start = ((), (), s32[]{:S(2)}) async-start(), calls=%async_computation.6 | async-start | bytes 2359296 | tf_op jit(solution)/shard_map/all_gather | solution.py:280
  13.0 180.2 %all-gather.34.cloned.1.call-start = ((), (), s32[]{:S(2)}) async-start(), calls=%async_computation.7 | async-start | bytes 2359296 | tf_op jit(solution)/shard_map/all_gather | solution.py:280
  13.6 208.5 %all-gather.36.cloned.1.call-start = ((), (), s32[]{:S(2)}) async-start(), calls=%async_computation.8 | async-start | bytes 2359296 | tf_op jit(solution)/shard_map/all_gather | solution.py:280
  14.3 246.3 %all-gather.38.cloned.1.call-start = ((), (), s32[]{:S(2)}) async-start(), calls=%async_computation.9 | async-start | bytes 2359296 | tf_op jit(solution)/shard_map/all_gather | solution.py:280
  15.1 293.2 %all-gather.40.cloned.1.call-start = ((), (), s32[]{:S(2)}) async-start(), calls=%async_computation.10 | async-start | bytes 9437184 | tf_op jit(solution)/shard_map/all_gather | solution.py:280
  15.8 348.6 %all-gather.42.cloned.1.call-start = ((), (), s32[]{:S(2)}) async-start(), calls=%async_computation.11 | async-start | bytes 9437184 | tf_op jit(solution)/shard_map/all_gather | solution.py:280
  15.9 81.7 %collective-permute-start.8 = (bf16[256,1024]{1,0:T(8,128)(2,1)}, bf16[256,1024]{1,0:T(8,128)(2,1)}, u32[]{:S(2)}, u32[]{:S(2)}) collective-permute-start(bf16[256,1024]{1,0:T(8,128)(2,1)} %bitcast.18), channel_id=1, source_target_pairs={{0,3},{1,0},{2,1},{3,2},{4,7},{5,4},{6,5},{7,6},{8,11},{9,8},{10,9... | collective-permute-start | bytes 1572872 | tf_op jit(solution)/shard_map/ppermute | solution.py:277
  21.0 76.6 %collective-permute-start.7 = (bf16[256,1024]{1,0:T(8,128)(2,1)}, bf16[256,1024]{1,0:T(8,128)(2,1)}, u32[]{:S(2)}, u32[]{:S(2)}) collective-permute-start(bf16[256,1024]{1,0:T(8,128)(2,1)} %bitcast.18), channel_id=1, source_target_pairs={{0,2},{1,3},{2,0},{3,1},{4,6},{5,7},{6,4},{7,5},{8,10},{9,11},{10,... | collective-permute-start | bytes 1572872 | tf_op jit(solution)/shard_map/ppermute | solution.py:277
  21.0 76.6 %collective-permute-start.6 = (bf16[256,1024]{1,0:T(8,128)(2,1)}, bf16[256,1024]{1,0:T(8,128)(2,1)}, u32[]{:S(2)}, u32[]{:S(2)}) collective-permute-start(bf16[256,1024]{1,0:T(8,128)(2,1)} %bitcast.18), channel_id=1, source_target_pairs={{0,1},{1,2},{2,3},{3,0},{4,5},{5,6},{6,7},{7,4},{8,9},{9,10},{10,1... | collective-permute-start | bytes 1572872 | tf_op jit(solution)/shard_map/ppermute | solution.py:277
  22.0 69.5 %collective-permute-start = (bf16[384,1024]{1,0:T(8,128)(2,1)}, bf16[384,1024]{1,0:T(8,128)(2,1)}, u32[]{:S(2)}, u32[]{:S(2)}) collective-permute-start(bf16[384,1024]{1,0:T(8,128)(2,1)} %bitcast.302), channel_id=1, source_target_pairs={{0,1},{1,2},{2,3},{4,5},{5,6},{6,7},{8,9},{9,10},{10,11},{12,13},{... | collective-permute-start | bytes 2359304 | tf_op jit(solution)/shard_map/ppermute | solution.py:271
  27.3 44.6 %collective-permute-start.3 = (s32[384]{0:T(512)S(1)}, s32[384]{0:T(512)S(1)}, u32[]{:S(2)}, u32[]{:S(2)}) collective-permute-start(s32[384]{0:T(512)S(1)} %reduce.1), channel_id=1, source_target_pairs={{0,1},{1,2},{2,3},{4,5},{5,6},{6,7},{8,9},{9,10},{10,11},{12,13},{... | collective-permute-start | bytes 4616 | tf_op jit(solution)/shard_map/ppermute | solution.py:271
  28.6 530.7 %all-reduce.3.cloned.1.call-start = ((), (), s32[]{:S(2)}) async-start(), calls=%async_computation | async-start | bytes 1703936 | tf_op jit(solution)/shard_map/psum | solution.py:388
  91.4 19.7 %collective-permute-start.1 = (bf16[384,1024]{1,0:T(8,128)(2,1)}, bf16[384,1024]{1,0:T(8,128)(2,1)}, u32[]{:S(2)}, u32[]{:S(2)}) collective-permute-start(bf16[384,1024]{1,0:T(8,128)(2,1)} %collective-permute-done), channel_id=1, source_target_pairs={{0,1},{1,2},{2,3},{4,5},{5,6},{6,7},{8,9},{9,10},{10,11},{12,13},{... | collective-permute-start | bytes 2359304 | tf_op jit(solution)/shard_map/ppermute | solution.py:271
  491.6 180.6 %all-gather.22.cloned.1.call-start = ((), (), s32[]{:S(2)}) async-start(), calls=%async_computation.1 | async-start | bytes 7667712 | tf_op jit(solution)/shard_map/all_gather | solution.py:389
  579.8 20.0 %collective-permute-start.9 = (bf16[384,1024]{1,0:T(8,128)(2,1)S(1)}, bf16[384,1024]{1,0:T(8,128)(2,1)S(1)}, u32[]{:S(2)}, u32[]{:S(2)}) collective-permute-start(bf16[384,1024]{1,0:T(8,128)(2,1)S(1)} %slice.231), channel_id=1, source_target_pairs={{1,0},{2,1},{3,2},{5,4},{6,5},{7,6},{9,8},{10,9},{11,10},{13,12},{... | collective-permute-start | bytes 2359304 | tf_op jit(solution)/shard_map/ppermute | solution.py:274
  600.1 35.5 %collective-permute-start.10 = (bf16[384,1024]{1,0:T(8,128)(2,1)S(1)}, bf16[384,1024]{1,0:T(8,128)(2,1)S(1)}, u32[]{:S(2)}, u32[]{:S(2)}) collective-permute-start(bf16[384,1024]{1,0:T(8,128)(2,1)S(1)} %fusion.53), channel_id=1, source_target_pairs={{1,0},{2,1},{3,2},{5,4},{6,5},{7,6},{9,8},{10,9},{11,10},{13,12},{... | collective-permute-start | bytes 2359304 | tf_op jit(solution)/shard_map/ppermute | solution.py:274
  602.5 35.3 %collective-permute-start.14 = (bf16[256,1024]{1,0:T(8,128)(2,1)S(1)}, bf16[256,1024]{1,0:T(8,128)(2,1)S(1)}, u32[]{:S(2)}, u32[]{:S(2)}) collective-permute-start(bf16[256,1024]{1,0:T(8,128)(2,1)S(1)} %get-tuple-element.40), channel_id=1, source_target_pairs={{0,1},{1,2},{2,3},{3,0},{4,5},{5,6},{6,7},{7,4},{8,9},{9,10},{10,1... | collective-permute-start | bytes 1572872 | tf_op jit(solution)/shard_map/ppermute | solution.py:277
  605.2 51.7 %collective-permute-start.13 = (bf16[256,1024]{1,0:T(8,128)(2,1)S(1)}, bf16[256,1024]{1,0:T(8,128)(2,1)S(1)}, u32[]{:S(2)}, u32[]{:S(2)}) collective-permute-start(bf16[256,1024]{1,0:T(8,128)(2,1)S(1)} %get-tuple-element.41), channel_id=1, source_target_pairs={{0,2},{1,3},{2,0},{3,1},{4,6},{5,7},{6,4},{7,5},{8,10},{9,11},{10,... | collective-permute-start | bytes 1572872 | tf_op jit(solution)/shard_map/ppermute | solution.py:277
  606.8 50.0 %collective-permute-start.12 = (bf16[256,1024]{1,0:T(8,128)(2,1)S(1)}, bf16[256,1024]{1,0:T(8,128)(2,1)S(1)}, u32[]{:S(2)}, u32[]{:S(2)}) collective-permute-start(bf16[256,1024]{1,0:T(8,128)(2,1)S(1)} %get-tuple-element.39), channel_id=1, source_target_pairs={{0,3},{1,0},{2,1},{3,2},{4,7},{5,4},{6,5},{7,6},{8,11},{9,8},{10,9... | collective-permute-start | bytes 1572872 | tf_op jit(solution)/shard_map/ppermute | solution.py:277
  635.8 33.9 %collective-permute-start.11 = (bf16[384,1024]{1,0:T(8,128)(2,1)S(1)}, bf16[384,1024]{1,0:T(8,128)(2,1)S(1)}, u32[]{:S(2)}, u32[]{:S(2)}) collective-permute-start(bf16[384,1024]{1,0:T(8,128)(2,1)S(1)} %fusion.54), channel_id=1, source_target_pairs={{1,0},{2,1},{3,2},{5,4},{6,5},{7,6},{9,8},{10,9},{11,10},{13,12},{... | collective-permute-start | bytes 2359304 | tf_op jit(solution)/shard_map/ppermute | solution.py:274
  (61 other events, 510.1 us)
Sparse Core Ops, SparseCore 0:
  10.5 30.6 all-gather.23
  43.7 27.8 all-gather.25
  74.1 27.8 all-gather.27
  103.8 27.9 all-gather.29
  134.0 27.8 all-gather.31
  163.7 27.8 all-gather.33
  194.1 27.8 all-gather.35
  223.9 27.8 all-gather.37
  253.8 54.4 all-gather.39
  310.0 54.3 all-gather.41
  491.7 67.5 all-reduce.2
  561.2 46.8 all-gather.21

commit v2 on v1

v2 whole, which is shorter than its diff:
```python
import functools

import jax
import jax.numpy as jnp
from jax import lax
from jax.experimental import pallas as pl
from jax.experimental.pallas import tpu as pltpu
from jax.sharding import Mesh
from jax.sharding import PartitionSpec as P

HEAD = 64
PAIR = 2 * HEAD
RANK = 16
AUG = 16
TERMS = 3
SEG_KINDS = 5
COLS = 256
NORM_EPS = 1e-05
FAR = -1e30
SCALE = HEAD**-0.5
F32 = jnp.float32
BF16 = jnp.bfloat16
ANY = pl.BlockSpec(memory_space=pltpu.HBM)
WHOLE = pl.BlockSpec(memory_space=pltpu.VMEM)


def dot(left, right, left_dim, right_dim):
    return lax.dot_general(left, right, (((left_dim,), (right_dim,)), ((), ())), preferred_element_type=F32)


def nn(left, right):
    return dot(left, right, 1, 0)


def nt(left, right):
    return dot(left, right, 1, 1)


def tn(left, right):
    return dot(left, right, 0, 0)


def params(mib):
    return pltpu.CompilerParams(vmem_limit_bytes=mib * 1024 * 1024)


def cost(flops, moved, exps=0):
    return pl.CostEstimate(flops=int(flops), bytes_accessed=int(moved), transcendentals=int(exps))


def each(total, size, body, unroll=4):
    def step(at, carry):
        body(pl.ds(pl.multiple_of(at * size, size), size))
        return carry

    lax.fori_loop(0, total // size, step, 0, unroll=min(unroll, total // size))


def fetch(refs, layout, own, rows, part, target, sems):
    copies = []
    for ref, entries in zip(refs, layout):
        for source, flip, who, first, count in entries:
            low, high = max(first, part * rows), min(first + count, (part + 1) * rows)
            if low < high:
                shard = own ^ who if flip else who
                copies.append(
                    pltpu.make_async_copy(
                        ref.at[pl.ds(source + low - first, high - low)],
                        target.at[pl.ds(pl.multiple_of(shard * rows + (low - part * rows), 16), high - low)],
                        sems.at[len(copies)],
                    )
                )
    return copies


def start_all(copies):
    for copy in copies:
        copy.start()


def wait_all(copies):
    for copy in copies:
        copy.wait()


def low_half(shape, axis):
    return lax.broadcasted_iota(jnp.int32, shape, axis) < HEAD


def split_pair(rows):
    low = low_half(rows.shape, 1)
    zero = jnp.zeros_like(rows)
    return jnp.concatenate([jnp.where(low, rows, zero), jnp.where(low, zero, rows)], axis=0)


def split_pair_t(cols):
    low = low_half(cols.shape, 0)
    zero = jnp.zeros_like(cols)
    return jnp.concatenate([jnp.where(low, cols, zero), jnp.where(low, zero, cols)], axis=1)


def join_pair_t(cols):
    half = cols.shape[1] // 2
    return jnp.where(low_half((PAIR, half), 0), cols[:, :half], cols[:, half:])


def turned(rows):
    return rows.astype(F32).T


def term_rows(row, rest):
    high = row.astype(BF16).astype(F32)
    mid = (row - high).astype(BF16).astype(F32)
    low = row - high - mid
    at = lax.broadcasted_iota(jnp.int32, rest.shape, 0)
    return jnp.where(at == 0, high, jnp.where(at == 1, mid, jnp.where(at == 2, low, rest))).astype(BF16)


def causal_scores(scores):
    keys, columns = scores.shape
    row = lax.broadcasted_iota(jnp.int32, (keys, columns // 2), 0)
    col = lax.broadcasted_iota(jnp.int32, (keys, columns // 2), 1)
    keep = row <= col
    return jnp.where(jnp.concatenate([keep, keep], axis=1), scores, FAR)


def out_slopes(grads, outs):
    gt = turned(grads)
    products = gt * turned(outs)
    delta = jnp.concatenate([jnp.sum(products[:HEAD], axis=0, keepdims=True), jnp.sum(products[HEAD:], axis=0, keepdims=True)], axis=1)
    rest = jnp.zeros((AUG, delta.shape[1]), F32)
    return jnp.concatenate([split_pair_t(gt.astype(BF16)), term_rows(-delta, rest)], axis=0)


def block_back(keys, values, kaug, qa, ga, q, grads, diagonal):
    scores = nn(jnp.concatenate([keys, kaug], axis=1), qa)
    if diagonal:
        scores = causal_scores(scores)
    chances = jnp.exp(scores)
    slopes = nn(jnp.concatenate([values, kaug], axis=1), ga)
    low_slopes = (chances * slopes).astype(BF16)
    grad_values = nn(chances.astype(BF16), grads).astype(BF16)
    grad_keys = nn(low_slopes, q).astype(BF16)
    grad_q = join_pair_t(nn(turned(keys).astype(BF16), low_slopes))
    return grad_q, grad_keys, grad_values


def slope_rows(ga_ref, do_ref, o_ref):
    for at in range(ga_ref.shape[0]):
        cols = slice(at * PAIR, (at + 1) * PAIR)
        ga_ref[at] = out_slopes(do_ref[:, cols], o_ref[:, cols])


def adapter_spec(first, count, width):
    return pl.BlockSpec((1, count, 1, RANK, width), lambda *at: (0, first // count, at[-1][2], 0, 0))


def mlp_adapter_spec(width):
    return pl.BlockSpec((1, 1, RANK, width), lambda *at: (0, at[-1][2], 0, 0))


def low_rank(rows, table):
    return nt(rows, table).astype(BF16)


class Gathered:
    def __init__(self, arrays, layout, rows):
        self.arrays, self.layout, self.rows = arrays, layout, rows
        self.count = sum(len(entries) for entries in layout)

    def bring(self, refs, own, part, target, sems):
        return fetch(refs, self.layout, own, self.rows, part, target, sems)

    def specs(self):
        return [ANY] * len(self.arrays)

    def sems(self, parts):
        return pltpu.SemaphoreType.DMA((parts, self.count))


def project_into(out_ref, rows, weight, hidden, up):
    def body(cols):
        out_ref[:, cols] = (nn(rows, weight[:, cols]) + nn(hidden, up(cols))).astype(out_ref.dtype)

    each(out_ref.shape[1], COLS, body)


class Gathered:
    def __init__(self, arrays, layout, rows):
        self.arrays, self.layout, self.rows = arrays, layout, rows
        self.count = sum(len(entries) for entries in layout)

    def bring(self, refs, own, part, target, sems):
        return fetch(refs, self.layout, own, self.rows, part, target, sems)

    def specs(self):
        return [ANY] * len(self.arrays)

    def sems(self, parts):
        return pltpu.SemaphoreType.DMA((parts, self.count))


def project_into(out_ref, rows, weight, hidden, up):
    def body(cols):
        out_ref[:, cols] = (nn(rows, weight[:, cols]) + nn(hidden, up(cols))).astype(out_ref.dtype)

    each(out_ref.shape[1], COLS, body)


class Step:
    def __init__(self, name, w, parts, at, first, last, causal):
        self.name, self.w, self.parts, self.at, self.first, self.last, self.causal = name, w, parts, at, first, last, causal
        self.diagonal = causal and at == 0

    def active(self, sc_ref):
        return sc_ref[0] >= self.at if self.causal and self.at else None

    def when(self, sc_ref, condition=None):
        conditions = [c for c in (self.active(sc_ref), condition) if c is not None]
        if not conditions:
            return lambda body: body()
        return pl.when(conditions[0] if len(conditions) == 1 else conditions[0] & conditions[1])


def head_cols():
    return pl.ds(pl.multiple_of(pl.program_id(0) * PAIR, PAIR), PAIR)


def attend_step_kernel(step, count, sc_ref, *refs):
    refs = list(refs)
    make_q = step.causal and step.first

    def take(number):
        return [refs.pop(0) for _ in range(number)]

    xs = take(count)
    a_ref, b_ref, kaug_ref = take(3)
    q_ref = take(1)[0] if step.first and not make_q else None
    seg_ref = take(1)[0] if step.first else None
    qa_in, acc_in, m_in = (None, None, None) if step.first else take(3)
    pieces = take(len(step.w.arrays))
    q_out = take(1)[0] if make_q else None
    k_out, v_out, r_out = take(3)
    o_out, qa_out = None, None
    if step.first:
        qa_out = take(1)[0]
    if step.last:
        o_out, qa_out, w_ref, k_all, v_all, sems, acc_ref, m_ref = take(8)
    else:
        acc_ref, m_ref, w_ref, k_all, v_all, sems = take(6)
        acc_ref, m_ref = acc_ref.at[0], m_ref.at[0]
    q_all = take(1)[0] if make_q else None
    parts = step.parts
    kinds = len(parts)

    @step.when(sc_ref, pl.program_id(0) == 0)
    def _():
        copies = [step.w.bring(pieces, sc_ref[1], part, w_ref.at[at], sems.at[at]) for at, part in enumerate(parts)]
        for part in copies:
            start_all(part)
        low = 0
        tables = a_ref[...].reshape(-1, a_ref.shape[-1])
        for x_ref in xs:
            x = x_ref[...]
            span = pl.ds(low, x.shape[0])
            low += x.shape[0]
            hidden = low_rank(x, tables)
            r_out[span, :] = hidden
            outs = [k_all, v_all]
            if make_q:
                outs.insert(0, q_all)
            for at, out in enumerate(outs):
                slot = at + a_ref.shape[1] - len(outs)
                own = hidden[:, slot * RANK : (slot + 1) * RANK]
                if x_ref is xs[0]:
                    wait_all(copies[at])

                def body(cols, at=at, slot=slot, own=own, out=out):
                    out[span, cols] = (nn(x, w_ref[at, :, cols]) + nn(own, b_ref[0, slot, 0, :, cols])).astype(BF16)

                each(out.shape[1], COLS, body)

    @step.when(sc_ref)
    def _():
        cols = head_cols()
        keys, values = k_all[:, cols], v_all[:, cols]
        k_out[...] = keys
        v_out[...] = values
        if step.first:
            q = q_all[:, cols] if make_q else q_ref[...]
            if make_q:
                q_out[...] = q
            seg = seg_ref[...]
            qt = split_pair_t((turned(q) * SCALE).astype(BF16))
            qa = jnp.concatenate([qt, jnp.concatenate([seg, seg], axis=1).astype(BF16)], axis=0)
            if not step.last:
                qa_out[0] = qa
        else:
            qa = qa_in[0]
        scores = nn(jnp.concatenate([keys, kaug_ref[...]], axis=1), qa)
        if step.diagonal:
            scores = causal_scores(scores)
        top = jnp.max(scores, axis=0, keepdims=True)
        vt = jnp.concatenate([turned(values).astype(BF16), jnp.ones((16, keys.shape[0]), BF16)], axis=0)
        if step.first:
            acc_ref[...] = nn(vt, jnp.exp(scores - top).astype(BF16))
        else:
            old = m_in[0, 0:1]
            top = jnp.maximum(old, top)
            acc_ref[...] = acc_in[0] * jnp.exp(old - top) + nn(vt, jnp.exp(scores - top).astype(BF16))
        m_ref[...] = jnp.broadcast_to(top, m_ref.shape)

    if step.active(sc_ref) is not None:

        @pl.when(jnp.logical_not(step.active(sc_ref)))
        def _():
            acc_ref[...] = acc_in[0]
            m_ref[...] = m_in[0]

    if step.last:
        total = acc_ref[PAIR : PAIR + 1]
        o_out[...] = join_pair_t(acc_ref[:PAIR] / total).T.astype(BF16)
        lse = m_ref[0:1] + jnp.log(total)
        qa = qa_in[0]
        qa_out[0] = jnp.concatenate([qa[:PAIR], term_rows(-lse, qa[PAIR:].astype(F32))], axis=0)


def attend_step(step, scalars, xs, tokens, block_rows, proj_down, proj_up, kaug, q, seg, state):
    width = xs[0].shape[1]
    pairs = width // PAIR
    keys = block_rows * len(xs)
    make_q = step.causal and step.first
    kinds = len(step.parts)
    slots = 3 if step.causal else 2
    by_head = pl.BlockSpec((tokens, PAIR), lambda h, s: (0, h))
    keys_by_head = pl.BlockSpec((keys, PAIR), lambda h, s: (0, h))
    extended = pl.BlockSpec((1, PAIR + AUG, 2 * tokens), lambda h, s: (h, 0, 0))
    m_spec = pl.BlockSpec((1, 8, 2 * tokens), lambda h, s: (h, 0, 0))
    adapters = adapter_spec(0 if step.causal else 4, slots, width)
    q_shape = jax.ShapeDtypeStruct((tokens, width), BF16)
    kv_shape = jax.ShapeDtypeStruct((keys, width), BF16)
    qa_shape = jax.ShapeDtypeStruct((pairs, PAIR + AUG, 2 * tokens), BF16)
    state_shapes = [jax.ShapeDtypeStruct((pairs, PAIR + 16, 2 * tokens), F32), jax.ShapeDtypeStruct((pairs, 8, 2 * tokens), F32)]
    in_specs = [pl.BlockSpec((block_rows, width), lambda h, s: (0, 0))] * len(xs)
    in_specs += [adapters, adapters, pl.BlockSpec((keys, AUG), lambda h, s: (0, 0))]
    args = [*xs, proj_down, proj_up, kaug]
    if step.first and not make_q:
        in_specs.append(by_head)
        args.append(q)
    if step.first:
        in_specs.append(pl.BlockSpec((AUG, tokens), lambda h, s: (0, 0)))
        args.append(seg)
    else:
        in_specs += [extended, extended, m_spec]
        args += state
    out_specs = [keys_by_head, keys_by_head, pl.BlockSpec((keys, slots * RANK), lambda h, s: (0, 0))]
    out_shape = [kv_shape, kv_shape, jax.ShapeDtypeStruct((keys, slots * RANK), BF16)]
    if make_q:
        out_specs.insert(0, by_head)
        out_shape.insert(0, q_shape)
    scratch = [pltpu.VMEM((kinds, width, width), BF16), pltpu.VMEM((keys, width), BF16), pltpu.VMEM((keys, width), BF16), step.w.sems(kinds)]
    if step.first:
        out_specs.append(extended)
        out_shape.append(qa_shape)
    if step.last:
        out_specs += [by_head, extended]
        out_shape += [q_shape, qa_shape]
        scratch += [pltpu.VMEM((PAIR + 16, 2 * tokens), F32), pltpu.VMEM((8, 2 * tokens), F32)]
    else:
        out_specs += [extended, m_spec]
        out_shape += state_shapes
    if make_q:
        scratch.append(pltpu.VMEM((tokens, width), BF16))
    call = pl.pallas_call(
        functools.partial(attend_step_kernel, step, len(xs)),
        grid_spec=pltpu.PrefetchScalarGridSpec(
            num_scalar_prefetch=1, grid=(pairs,), in_specs=in_specs + step.w.specs(), out_specs=out_specs, scratch_shapes=scratch
        ),
        out_shape=out_shape,
        name=step.name,
        compiler_params=params(60),
        cost_estimate=cost(4 * tokens * keys * width + 2 * kinds * keys * width * width, 20 * tokens * width, tokens * keys * width // HEAD),
    )
    return list(call(scalars, *args, *step.w.arrays))


def back_step_kernel(step, count, sc_ref, *refs):
    refs = list(refs)

    def take(number):
        return [refs.pop(0) for _ in range(number)]

    qa_ref, ga_ref, q_ref, do_ref, k_ref, v_ref, kaug_ref, r_ref, a_ref, b_ref = take(10)
    xs = take(count)
    dqt_in, sums_in = (None, None) if step.first else take(2)
    query = step.causal and step.last
    d1_ref = take(1)[0] if query else None
    pieces = take(len(step.w.arrays))
    dq_all = None
    if query:
        base_ref, grads_ref, w_ref, dk_all, dv_all, sems, dq_all = refs
    elif step.last:
        own_ref, part_ref, dq_ref, grads_ref, w_ref, dk_all, dv_all, sems = refs
    else:
        part_ref, dqt_ref, sums_ref, w_ref, dk_all, dv_all, sems = refs
    h = pl.program_id(0)
    final = h == pl.num_programs(0) - 1
    width = a_ref.shape[-1]
    parts = step.parts
    slots = a_ref.shape[1]

    def weights():
        return [step.w.bring(pieces, sc_ref[1], part, w_ref.at[at], sems.at[at]) for at, part in enumerate(parts)]

    @step.when(sc_ref, h == 0)
    def _():
        for part in weights():
            start_all(part)

    @step.when(sc_ref)
    def _():
        q = split_pair(q_ref[...] * jnp.asarray(SCALE, BF16))
        grad_q, grad_keys, grad_values = block_back(
            k_ref[...], v_ref[...], kaug_ref[...], qa_ref[0], ga_ref[0], q, split_pair(do_ref[...]), step.diagonal
        )
        cols = head_cols()
        dk_all[:, cols] = grad_keys
        dv_all[:, cols] = grad_values
        if not step.first:
            grad_q = grad_q + dqt_in[0]
        if query:
            dq_all[:, cols] = (grad_q * SCALE).T.astype(BF16)
        elif step.last:
            dq_ref[...] = (grad_q * SCALE).T.astype(BF16)
        else:
            dqt_ref[0] = grad_q

    if step.active(sc_ref) is not None:

        @pl.when(jnp.logical_not(step.active(sc_ref)))
        def _():
            dqt_ref[0] = jnp.zeros_like(dqt_ref[0]) if step.first else dqt_in[0]

            @pl.when(final)
            def _():
                part_ref[...] = jnp.zeros_like(part_ref)
                sums_ref[...] = jnp.zeros_like(sums_ref) if step.first else sums_in[...]

    @step.when(sc_ref, final)
    def _():
        grads = [dq_all, dk_all, dv_all] if query else [dk_all, dv_all]
        shift = slots - len(grads)
        drs, dbs = [], []
        hidden = r_ref[...]
        for at, grad_ref in enumerate(grads):
            slot = at + shift
            grad = grad_ref[...]
            drs.append(low_rank(grad, b_ref[0, slot, 0]))
            dbs.append(tn(hidden[:, slot * RANK : (slot + 1) * RANK], grad))
        dr = jnp.concatenate(drs, axis=1)
        low, da = 0, None
        for x_ref in xs:
            part = tn(dr[low : low + x_ref.shape[0]], x_ref[...])
            da = part if da is None else da + part
            low += x_ref.shape[0]
        olds = [None] * 4 if step.first else [sums_in[at * RANK : (at + 1) * RANK] for at in range(4)]
        if query:
            olds = [None, *olds[:2], None, *olds[2:]]
        total = [da[at * RANK : (at + 1) * RANK] for at in range(len(grads))] + dbs
        target = grads_ref if step.last else sums_ref
        for at, (new, old) in enumerate(zip(total, olds)):
            target[at * RANK : (at + 1) * RANK] = (new if old is None else new + old).astype(target.dtype)
        for part in weights():
            wait_all(part)
        rows = dk_all.shape[0]
        own = rows // count if step.last and not query else 0

        def body(cols):
            table = a_ref[0, shift:, 0, :, cols].reshape(len(grads) * RANK, COLS)
            value = nn(dr, table)
            for at, grad_ref in enumerate(grads):
                value = value + nt(grad_ref[...], w_ref[at, cols, :])
            if query:
                base_ref[:, cols] = value + d1_ref[:, cols]
            elif step.last:
                own_ref[:, cols] = value[:own]
                part_ref[:, cols] = value[own:].astype(BF16)
            else:
                part_ref[:, cols] = value.astype(BF16)

        each(width, COLS, body)


def back_step(step, scalars, qa, ga, q, do, k, v, kaug, r, xs, block_rows, proj_down, proj_up, state, d1):
    tokens, width = q.shape
    pairs = width // PAIR
    keys = k.shape[0]
    slots = 3 if step.causal else 2
    query = step.causal and step.last
    by_head = pl.BlockSpec((tokens, PAIR), lambda h, s: (0, h))
    keys_by_head = pl.BlockSpec((keys, PAIR), lambda h, s: (0, h))
    extended = pl.BlockSpec((1, PAIR + AUG, 2 * tokens), lambda h, s: (h, 0, 0))
    dqt_spec = pl.BlockSpec((1, PAIR, tokens), lambda h, s: (h, 0, 0))

    def whole(rows):
        return pl.BlockSpec((rows, width), lambda h, s: (0, 0))

    adapters = adapter_spec(0 if step.causal else 4, slots, width)
    in_specs = [
        extended,
        extended,
        by_head,
        by_head,
        keys_by_head,
        keys_by_head,
        pl.BlockSpec((keys, AUG), lambda h, s: (0, 0)),
        pl.BlockSpec((keys, slots * RANK), lambda h, s: (0, 0)),
        adapters,
        adapters,
        *[whole(block_rows)] * len(xs),
    ]
    args = [qa, ga, q, do, k, v, kaug, r, proj_down, proj_up, *xs]
    if not step.first:
        in_specs += [dqt_spec, whole(4 * RANK)]
        args += state
    scratch = [pltpu.VMEM((len(step.parts), width, width), BF16), pltpu.VMEM((keys, width), BF16), pltpu.VMEM((keys, width), BF16)]
    scratch.append(step.w.sems(len(step.parts)))
    if query:
        in_specs.append(whole(tokens))
        args.append(d1)
        scratch.append(pltpu.VMEM((tokens, width), BF16))
        out_specs = [whole(tokens), whole(6 * RANK)]
        out_shape = [jax.ShapeDtypeStruct((tokens, width), F32), jax.ShapeDtypeStruct((6 * RANK, width), BF16)]
    elif step.last:
        rest = keys - block_rows
        out_specs = [whole(block_rows), whole(rest), by_head, whole(4 * RANK)]
        out_shape = [
            jax.ShapeDtypeStruct((block_rows, width), F32),
            jax.ShapeDtypeStruct((rest, width), BF16),
            jax.ShapeDtypeStruct((tokens, width), BF16),
            jax.ShapeDtypeStruct((4 * RANK, width), BF16),
        ]
    else:
        out_specs = [whole(keys), dqt_spec, whole(4 * RANK)]
        out_shape = [
            jax.ShapeDtypeStruct((keys, width), BF16),
            jax.ShapeDtypeStruct((pairs, PAIR, tokens), F32),
            jax.ShapeDtypeStruct((4 * RANK, width), F32),
        ]
    return pl.pallas_call(
        functools.partial(back_step_kernel, step, len(xs)),
        grid_spec=pltpu.PrefetchScalarGridSpec(
            num_scalar_prefetch=1, grid=(pairs,), in_specs=in_specs + step.w.specs(), out_specs=out_specs, scratch_shapes=scratch
        ),
        out_shape=out_shape,
        name=step.name,
        compiler_params=params(60),
        cost_estimate=cost(10 * tokens * keys * width + 4 * keys * width * width, 24 * tokens * width, tokens * keys * width // HEAD),
    )(scalars, *args, *step.w.arrays)


ROWS = 64


def normalize_rows(u_ref, norm_ref, low_ref, std_ref):
    def body(rows):
        values = u_ref[rows, :]
        centered = values - jnp.mean(values, -1, keepdims=True)
        inv_std = lax.rsqrt(jnp.mean(centered * centered, -1, keepdims=True) + NORM_EPS)
        normed = centered * inv_std
        norm_ref[rows, :] = normed
        low_ref[rows, :] = normed.astype(BF16)
        std_ref[rows, :] = inv_std

    each(u_ref.shape[0], ROWS, body)


def normalize_back(grads, normed, inv_std):
    return inv_std * (grads - jnp.mean(grads, -1, keepdims=True) - normed * jnp.mean(grads * normed, -1, keepdims=True))


def mid_kernel(w, part, query, sc_ref, o_ref, x_ref, a_ref, b_ref, aq_ref, bq_ref, *refs):
    pieces, refs = refs[: len(w.arrays)], refs[len(w.arrays) :]
    if query:
        norm_ref, low_ref, std_ref, r_ref, q_ref, w_ref, u_ref, sems = refs
    else:
        norm_ref, low_ref, std_ref, r_ref, w_ref, u_ref, sems = refs
    width = x_ref.shape[1]
    first = w.bring(pieces, sc_ref[1], part, w_ref.at[0], sems.at[0])
    start_all(first)
    if query:
        second = w.bring(pieces, sc_ref[1], 2, w_ref.at[1], sems.at[1])
        start_all(second)
    o = o_ref[...]
    hidden = low_rank(o, a_ref[0, 0, 0])
    r_ref[:, :RANK] = hidden
    wait_all(first)

    def body(cols):
        u_ref[:, cols] = x_ref[:, cols].astype(F32) + nn(o, w_ref[0, :, cols]) + nn(hidden, b_ref[0, 0, 0, :, cols])

    each(width, COLS, body)
    normalize_rows(u_ref, norm_ref, low_ref, std_ref)
    if query:
        low = low_ref[...]
        hidden_q = low_rank(low, aq_ref[0, 0, 0])
        r_ref[:, RANK:] = hidden_q
        wait_all(second)
        project_into(q_ref, low, w_ref.at[1], hidden_q, lambda cols: bq_ref[0, 0, 0, :, cols])


def mid(name, scalars, outs, residual, part, proj, query, proj_down, proj_up, w):
    rows, width = outs.shape
    shapes = [
        jax.ShapeDtypeStruct((rows, width), F32),
        jax.ShapeDtypeStruct((rows, width), BF16),
        jax.ShapeDtypeStruct((rows, 1), F32),
        jax.ShapeDtypeStruct((rows, 2 * RANK if query else RANK), BF16),
    ]
    if query:
        shapes.append(jax.ShapeDtypeStruct((rows, width), BF16))
    spec, spec_q = adapter_spec(proj, 1, width), adapter_spec(3, 1, width)
    return pl.pallas_call(
        functools.partial(mid_kernel, w, part, query),
        grid_spec=pltpu.PrefetchScalarGridSpec(
            num_scalar_prefetch=1,
            grid=(1,),
            in_specs=[WHOLE, WHOLE, spec, spec, spec_q, spec_q, *w.specs()],
            out_specs=[WHOLE] * len(shapes),
            scratch_shapes=[pltpu.VMEM((2, width, width), BF16), pltpu.VMEM((rows, width), F32), w.sems(2)],
        ),
        out_shape=shapes,
        name=name,
        compiler_params=params(60),
        cost_estimate=cost(4 * rows * width * width, 12 * rows * width + 4 * width * width),
    )(scalars, outs, residual, proj_down, proj_up, proj_down, proj_up, *w.arrays)


def gelu_kernel(w, sc_ref, x_ref, a_ref, b_ref, *refs):
    pieces, (g_ref, slope_ref, r_ref, w_ref, sems) = refs[: len(w.arrays)], refs[len(w.arrays) :]
    copies = w.bring(pieces, sc_ref[1], 0, w_ref, sems.at[0])
    start_all(copies)
    x = x_ref[...]
    hidden = low_rank(x, a_ref[0, 0])
    r_ref[...] = hidden
    wait_all(copies)

    def body(cols):
        pre = nn(x, w_ref[:, cols]) + nn(hidden, b_ref[0, 0, :, cols])
        phi = 0.5 * (1.0 + lax.erf(pre * 0.7071067811865476))
        g_ref[:, cols] = (pre * phi).astype(BF16)
        slope_ref[:, cols] = (phi + pre * jnp.exp(-0.5 * pre * pre) * 0.3989422804014327).astype(BF16)

    each(g_ref.shape[1], COLS, body)


def gelu_up(scalars, x, down, up, w):
    rows, width = x.shape
    wide = up.shape[3]
    return pl.pallas_call(
        functools.partial(gelu_kernel, w),
        grid_spec=pltpu.PrefetchScalarGridSpec(
            num_scalar_prefetch=1,
            grid=(1,),
            in_specs=[WHOLE, mlp_adapter_spec(width), mlp_adapter_spec(wide), *w.specs()],
            out_specs=[WHOLE] * 3,
            scratch_shapes=[pltpu.VMEM((width, wide), BF16), w.sems(1)],
        ),
        out_shape=[
            jax.ShapeDtypeStruct((rows, wide), BF16),
            jax.ShapeDtypeStruct((rows, wide), BF16),
            jax.ShapeDtypeStruct((rows, RANK), BF16),
        ],
        name="gelu_up",
        compiler_params=params(60),
        cost_estimate=cost(2 * rows * width * wide, 2 * width * wide + 4 * rows * wide, 2 * rows * wide),
    )(scalars, x, down, up, *w.arrays)


FC_ROWS = {"da1": 0, "db1": 16, "da2": 80, "db2": 144, "da_co": 160, "db_co": 176, "pick": 192}
FC_TOTAL = 208


def mlp_kernel(w_up, w_down, w_mid, sc_ref, g_ref, slope_ref, h2_ref, h2_low_ref, std2_ref, cot_ref, r1_ref, rco_ref, oc_ref,
               a1_ref, b1_ref, a2_ref, b2_ref, a7_ref, b7_ref, *refs):
    ups, refs = refs[: len(w_up.arrays)], refs[len(w_up.arrays) :]
    downs, refs = refs[: len(w_down.arrays)], refs[len(w_down.arrays) :]
    mids, refs = refs[: len(w_mid.arrays)], refs[len(w_mid.arrays) :]
    y_ref, d2_ref, doc_ref, gac_ref, grads_ref, w1, w2, wco, u, low, dpre, sem1, sem2, sem3 = refs
    rows, width = h2_ref.shape
    wide = g_ref.shape[1]
    own = sc_ref[1]
    copies2 = w_down.bring(downs, own, 0, w2, sem2.at[0])
    copies1 = w_up.bring(ups, own, 0, w1, sem1.at[0])
    copies3 = w_mid.bring(mids, own, 1, wco, sem3.at[0])
    start_all(copies2)
    start_all(copies1)
    start_all(copies3)
    g = g_ref[...]
    r2 = low_rank(g, a2_ref[0, 0])
    wait_all(copies2)

    def second(cols):
        u[:, cols] = h2_ref[:, cols] + nn(g_ref[...], w2[:, cols]) + nn(r2, b2_ref[0, 0, :, cols])

    each(width, COLS, second)

    def third(at):
        values = u[at, :]
        centered = values - jnp.mean(values, -1, keepdims=True)
        inv_std = lax.rsqrt(jnp.mean(centered * centered, -1, keepdims=True) + NORM_EPS)
        normed = centered * inv_std
        y_ref[at, :] = normed.astype(BF16)
        d3 = normalize_back(cot_ref[at, :].astype(F32), normed, inv_std)
        u[at, :] = d3
        low[at, :] = d3.astype(BF16)

    each(rows, ROWS, third)
    d3_low = low[...]
    grads_ref[pl.ds(FC_ROWS["db2"], RANK), :] = tn(r2, d3_low).astype(BF16)
    dr2 = low_rank(d3_low, b2_ref[0, 0])
    r1 = r1_ref[...]
    run = 2 * COLS
    runs = width // run

    def slopes(at, carry):
        cols = pl.ds(pl.multiple_of(at * run, run), run)
        down_rows = nt(low[...], w2[cols, :]) + nn(dr2, a2_ref[0, 0, :, cols])
        part = (down_rows * slope_ref[:, cols].astype(F32)).astype(BF16)
        dpre[:, cols] = part
        row = pl.multiple_of((at // runs) * RANK, RANK)
        place = pl.ds(pl.multiple_of((at % runs) * run, run), run)
        grads_ref[pl.ds(FC_ROWS["da2"] + row, RANK), place] = tn(dr2, g_ref[:, cols]).astype(BF16)
        grads_ref[pl.ds(FC_ROWS["db1"] + row, RANK), place] = tn(r1, part).astype(BF16)
        return carry

    lax.fori_loop(0, wide // run, slopes, 0)
    dr1 = low_rank(dpre[...], b1_ref[0, 0])
    grads_ref[pl.ds(FC_ROWS["da1"], RANK), :] = tn(dr1, h2_low_ref[...]).astype(BF16)
    wait_all(copies1)

    def first(cols):
        u[:, cols] += nt(dpre[...], w1[cols, :]) + nn(dr1, a1_ref[0, 0, :, cols])

    each(width, COLS, first)

    def norm(at):
        d2 = normalize_back(u[at, :], h2_ref[at, :], std2_ref[at, :])
        d2_ref[at, :] = d2
        low[at, :] = d2.astype(BF16)

    each(rows, ROWS, norm)
    wait_all(copies3)
    d2_low = low[...]
    grads_ref[pl.ds(FC_ROWS["db_co"], RANK), :] = tn(rco_ref[...], d2_low).astype(BF16)
    drc = low_rank(d2_low, b7_ref[0, 0, 0])
    grads_ref[pl.ds(FC_ROWS["da_co"], RANK), :] = tn(drc, oc_ref[...]).astype(BF16)

    def cross(cols):
        doc_ref[:, cols] = (nt(low[...], wco[cols, :]) + nn(drc, a7_ref[0, 0, 0, :, cols])).astype(BF16)

    each(width, COLS, cross)
    slope_rows(gac_ref, doc_ref, oc_ref)
    mine = jnp.where(sc_ref[0] == 0, sc_ref[2], 0).astype(F32)
    grads_ref[pl.ds(FC_ROWS["pick"], 16), :] = jnp.full((16, width), mine, F32).astype(BF16)


def mlp(scalars, g, slope, h2, h2_low, std2, cot, r1, rco, oc, fc1_down, fc1_up, fc2_down, fc2_up, proj_down, proj_up, w_up, w_down, w_mid):
    rows, width = h2.shape
    wide = g.shape[1]
    return pl.pallas_call(
        functools.partial(mlp_kernel, w_up, w_down, w_mid),
        grid_spec=pltpu.PrefetchScalarGridSpec(
            num_scalar_prefetch=1,
            grid=(1,),
            in_specs=[
                *[WHOLE] * 9,
                mlp_adapter_spec(width),
                mlp_adapter_spec(wide),
                mlp_adapter_spec(wide),
                mlp_adapter_spec(width),
                adapter_spec(7, 1, width),
                adapter_spec(7, 1, width),
                *w_up.specs(),
                *w_down.specs(),
                *w_mid.specs(),
            ],
            out_specs=[WHOLE] * 5,
            scratch_shapes=[
                pltpu.VMEM((width, wide), BF16),
                pltpu.VMEM((wide, width), BF16),
                pltpu.VMEM((width, width), BF16),
                pltpu.VMEM((rows, width), F32),
                pltpu.VMEM((rows, width), BF16),
                pltpu.VMEM((rows, wide), BF16),
                w_up.sems(1),
                w_down.sems(1),
                w_mid.sems(1),
            ],
        ),
        out_shape=[
            jax.ShapeDtypeStruct((rows, width), BF16),
            jax.ShapeDtypeStruct((rows, width), F32),
            jax.ShapeDtypeStruct((rows, width), BF16),
            jax.ShapeDtypeStruct((width // PAIR, PAIR + AUG, 2 * rows), BF16),
            jax.ShapeDtypeStruct((FC_TOTAL, width), BF16),
        ],
        name="mlp",
        compiler_params=params(60),
        cost_estimate=cost(6 * rows * width * wide, 4 * width * wide + 4 * rows * wide),
    )(scalars, g, slope, h2, h2_low, std2, cot, r1, rco, oc, fc1_down, fc1_up, fc2_down, fc2_up, proj_down, proj_up,
      *w_up.arrays, *w_down.arrays, *w_mid.arrays)


def mid_back_kernel(w, sc_ref, dqc_ref, d2_ref, h1_ref, h1_low_ref, std1_ref, r_ref, o_ref, aq_ref, bq_ref, a_ref, b_ref, *refs):
    pieces, refs = refs[: len(w.arrays)], refs[len(w.arrays) :]
    d1_ref, do_ref, ga_ref, grads_ref, w_ref, low, sems = refs
    rows, width = d2_ref.shape
    first = w.bring(pieces, sc_ref[1], 2, w_ref.at[1], sems.at[1])
    second = w.bring(pieces, sc_ref[1], 0, w_ref.at[0], sems.at[0])
    start_all(first)
    start_all(second)
    dqc = dqc_ref[...]
    drq = low_rank(dqc, bq_ref[0, 0, 0])
    grads_ref[0:RANK, :] = tn(drq, h1_low_ref[...]).astype(BF16)
    grads_ref[2 * RANK : 3 * RANK, :] = tn(r_ref[:, RANK:], dqc).astype(BF16)
    wait_all(first)

    def query(cols):
        d1_ref[:, cols] = d2_ref[:, cols] + nt(dqc_ref[...], w_ref[1, cols, :]) + nn(drq, aq_ref[0, 0, 0, :, cols])

    each(width, COLS, query)

    def norm(at):
        d1 = normalize_back(d1_ref[at, :], h1_ref[at, :], std1_ref[at, :])
        d1_ref[at, :] = d1
        low[at, :] = d1.astype(BF16)

    each(rows, ROWS, norm)
    wait_all(second)
    d1_low = low[...]
    dr = low_rank(d1_low, b_ref[0, 0, 0])
    grads_ref[RANK : 2 * RANK, :] = tn(dr, o_ref[...]).astype(BF16)
    grads_ref[3 * RANK :, :] = tn(r_ref[:, :RANK], d1_low).astype(BF16)

    def out(cols):
        do_ref[:, cols] = (nt(low[...], w_ref[0, cols, :]) + nn(dr, a_ref[0, 0, 0, :, cols])).astype(BF16)

    each(width, COLS, out)

    slope_rows(ga_ref, do_ref, o_ref)


def mid_back(scalars, dqc, d2, h1, h1_low, std1, r, o, proj_down, proj_up, w):
    rows, width = d2.shape
    spec, spec_q = adapter_spec(6, 1, width), adapter_spec(3, 1, width)
    return pl.pallas_call(
        functools.partial(mid_back_kernel, w),
        grid_spec=pltpu.PrefetchScalarGridSpec(
            num_scalar_prefetch=1,
            grid=(1,),
            in_specs=[*[WHOLE] * 7, spec_q, spec_q, spec, spec, *w.specs()],
            out_specs=[WHOLE] * 4,
            scratch_shapes=[pltpu.VMEM((2, width, width), BF16), pltpu.VMEM((rows, width), BF16), w.sems(2)],
        ),
        out_shape=[
            jax.ShapeDtypeStruct((rows, width), F32),
            jax.ShapeDtypeStruct((rows, width), BF16),
            jax.ShapeDtypeStruct((width // PAIR, PAIR + AUG, 2 * rows), BF16),
            jax.ShapeDtypeStruct((4 * RANK, width), BF16),
        ],
        name="mid_back",
        compiler_params=params(60),
        cost_estimate=cost(4 * rows * width * width, 20 * rows * width + 4 * width * width),
    )(scalars, dqc, d2, h1, h1_low, std1, r, o, proj_down, proj_up, proj_down, proj_up, *w.arrays)


def add_picked(picks_ref, sequences, out, source, first=0):
    adapters, view = out
    for adapter in range(adapters):
        view(adapter)[...] = jnp.zeros(view(adapter).shape, F32)
    for at in range(sequences):
        target = view(picks_ref[first + at])
        target[...] += source(at).astype(F32)


def fc_total_kernel(picks_ref, g_ref, a1_ref, b1_ref, a2_ref, b2_ref):
    sequences, _, width = g_ref.shape
    adapters = a1_ref.shape[1]

    def put(out_ref, col, row):
        def view(adapter):
            return out_ref.at[0, adapter, :, pl.ds(col, width)]

        add_picked(picks_ref, sequences, (adapters, view), lambda at: g_ref[at, pl.ds(row, RANK), :])

    for out_ref, name in ((a1_ref, "da1"), (b1_ref, "db1"), (a2_ref, "da2"), (b2_ref, "db2")):
        for at in range(out_ref.shape[3] // width):
            put(out_ref, at * width, FC_ROWS[name] + at * RANK)


def fc_total(picks, gathered, shapes):
    return pl.pallas_call(
        fc_total_kernel,
        grid_spec=pltpu.PrefetchScalarGridSpec(
            num_scalar_prefetch=1, grid=(1,), in_specs=[WHOLE], out_specs=[WHOLE] * 4
        ),
        out_shape=[jax.ShapeDtypeStruct(s, F32) for s in shapes],
        name="fc_total",
        compiler_params=params(60),
        cost_estimate=cost(0, 8 * 160 * 1024 * 6),
    )(picks, gathered)


PROJ_ROWS = {
    0: (2, 0, 48),
    1: (2, 16, 64),
    2: (2, 32, 80),
    3: (1, 0, 32),
    4: (1, 64, 96),
    5: (1, 80, 112),
    6: (1, 16, 48),
    7: (0, FC_ROWS["da_co"], FC_ROWS["db_co"]),
}


def proj_total_kernel(picks_ref, g0_ref, g1_ref, g2_ref, down_ref, up_ref):
    adapters = down_ref.shape[2]
    for proj, (source, down_row, up_row) in PROJ_ROWS.items():
        g_ref = (g0_ref, g1_ref, g2_ref)[source]

        @pl.when(pl.program_id(0) == proj)
        def _(g_ref=g_ref, down_row=down_row, up_row=up_row, source=source):
            for out_ref, row in ((down_ref, down_row), (up_ref, up_row)):
                add_picked(
                    picks_ref, g_ref.shape[0], (adapters, lambda adapter, out_ref=out_ref: out_ref.at[0, 0, adapter]),
                    lambda at, row=row: g_ref[at, pl.ds(row, RANK), :], g_ref.shape[0] if source == 2 else 0,
                )


def proj_total(picks, g0, g1, g2, shape):
    block = pl.BlockSpec((1, 1, *shape[2:]), lambda p, s: (0, p, 0, 0, 0))
    return pl.pallas_call(
        proj_total_kernel,
        grid_spec=pltpu.PrefetchScalarGridSpec(
            num_scalar_prefetch=1, grid=(shape[1],), in_specs=[WHOLE] * 3, out_specs=[block] * 2
        ),
        out_shape=[jax.ShapeDtypeStruct(shape, F32)] * 2,
        name="proj_total",
        compiler_params=params(60),
        cost_estimate=cost(0, 8 * 256 * 1024 * 6),
    )(picks, g0, g1, g2)


class Gathering:
    def __init__(self, shard, parts, across, sibling):
        self.shard, self.parts, self.across, self.sibling = shard, parts, across, sibling
        self.half = shard.shape[0] // 2

    def begin(self):
        self.x, self.y = self.across(self.shard, 1), self.across(self.shard, 2)
        self.own = self.sibling(self.shard)

    def forward(self):
        self.xy, self.yx = self.across(self.x[: self.half], 2), self.across(self.y[self.half :], 1)
        self.sx, self.sy = self.sibling(self.x), self.sibling(self.y)

    def share(self):
        self.sxy, self.syx = self.sibling(self.xy), self.sibling(self.yx)

    def result(self):
        rows, half = self.shard.shape[0], self.half
        arrays = [self.shard, self.own, self.x, self.sx, self.y, self.sy, self.xy, self.sxy, self.yx, self.syx]
        layout = [[(0, True, who, 0, rows)] for who in range(6)]
        layout += [[(0, True, who, 0, half)] for who in (6, 7)]
        layout += [[(0, True, who, half, rows - half)] for who in (6, 7)]
        return Gathered(arrays, layout, rows // self.parts)


class Whole:
    def __init__(self, shard, parts, shards, gather):
        self.shard, self.parts, self.shards, self.gather = shard, parts, shards, gather
        self.x = self.y = self.xy = self.yx = shard

    def begin(self):
        self.whole = self.gather(self.shard)

    def forward(self):
        pass

    def share(self):
        pass

    def result(self):
        rows = self.shard.shape[0]
        return Gathered([self.whole], [[(at * rows, False, at, 0, rows) for at in range(self.shards)]], rows // self.parts)


def make_shards(mesh):
    chips, span = mesh.shape["chip"], mesh.shape["sp"]
    plane = ("chip", "core")

    def tie(*values):
        return lax.optimization_barrier(values)

    def up(values):
        return lax.ppermute(values, "sp", [(i, i + 1) for i in range(span - 1)])

    def down(values):
        return lax.ppermute(values, "sp", [(i + 1, i) for i in range(span - 1)])

    def turn(values, by):
        return lax.ppermute(values, "sp", [(i, (i + by) % span) for i in range(span)])

    def swap(values, bit):
        return lax.ppermute(values, "sp", [(i, i ^ bit) for i in range(span)])

    def across(values, bit):
        return lax.ppermute(values, "chip", [(i, i ^ bit) for i in range(chips)])

    def sibling(values):
        return lax.ppermute(values, "core", [(0, 1), (1, 0)])

    def gathering(shard, parts):
        if chips == 4:
            return Gathering(shard, parts, across, sibling)
        return Whole(shard, parts, 2 * chips, lambda v: lax.all_gather(v, plane, axis=0, tiled=True))

    def everywhere(flat):
        flat = lax.psum(flat, "sp")
        return lax.all_gather(flat, plane, axis=0, tiled=False), flat

    def everywhere_now(flat):
        bit = 1
        while bit < span:
            flat = (flat.astype(F32) + swap(flat, bit).astype(F32)).astype(BF16)
            bit *= 2
        flat, bit = flat[None], 1
        while bit < chips:
            flat = jnp.concatenate([flat, across(flat, bit)], axis=0)
            bit *= 2
        return jnp.concatenate([flat, sibling(flat)], axis=0)

    order = [2 * at for at in range(chips)] + [2 * at + 1 for at in range(chips)]

    def shards(
        inputs,
        segments,
        enc_states,
        adapter_pick,
        qkv_weights,
        out_weights,
        mlp_in,
        mlp_out,
        proj_down,
        proj_up,
        fc1_down,
        fc1_up,
        fc2_down,
        fc2_up,
        cotangent,
    ):
        x_low = inputs[0]
        memory = enc_states[0]
        tokens, width = x_low.shape
        mem_rows = memory.shape[0]
        own = lax.axis_index("chip") * 2 + lax.axis_index("core")
        scalars = jnp.stack([lax.axis_index("sp"), own, adapter_pick[0]]).astype(jnp.int32)
        tables = (proj_down, proj_up)

        a = gathering(qkv_weights[0, :3].reshape(-1, width), 3)
        b = gathering(jnp.concatenate([out_weights[0].reshape(-1, width), qkv_weights[0, 3:].reshape(-1, width)], axis=0), 5)
        c, d = gathering(mlp_in[0], 1), gathering(mlp_out[0], 1)

        seg_row = jnp.pad(segments.astype(BF16), ((0, 15), (0, width - tokens)))
        ext = [jnp.concatenate([x_low, seg_row], axis=0)]
        lane = jnp.arange(AUG, dtype=jnp.int32)
        kinds = (lane >= TERMS) & (lane < TERMS + SEG_KINDS)
        q_seg = (kinds[:, None] & (lane[:, None] - TERMS == segments)).astype(F32)
        free_seg = jnp.zeros((AUG, tokens), F32)

        def key_aug(block):
            seg = block[tokens, :tokens].astype(jnp.int32)
            return jnp.where(lane[None] < TERMS, 1.0, jnp.where(kinds[None] & (lane[None] - TERMS != seg[:, None]), FAR, 0.0)).astype(BF16)

        half = span // 2
        halves = [range(half), range(half, span)]
        free_aug = jnp.broadcast_to((lane[None] < TERMS).astype(BF16), (half * mem_rows, AUG))

        ext.append(up(ext[0]))
        a.begin()
        downs, ups = [memory], [memory]
        downs.append(down(memory))
        ext[1], a.x, a.y, b.shard, downs[1] = tie(ext[1], a.x, a.y, b.shard, downs[1])
        ext.append(up(ext[1]))
        a.forward()
        b.begin()
        downs.append(down(downs[1]))
        a.xy, a.yx, downs[2] = tie(a.xy, a.yx, downs[2])
        a.share()
        while len(downs) < span:
            downs.append(down(downs[-1]))
        w_a = a.result()

        state, ks, vs, rs, augs = None, [], [], [], []
        q = qa = o = None
        for at in range(span):
            step = Step(f"self_{at}", w_a, (0, 1, 2) if at == 0 else (1, 2), at, at == 0, at == span - 1, True)
            augs.append(key_aug(ext[at]))
            out = attend_step(step, scalars, [ext[at]], tokens, tokens, *tables, augs[at], None, q_seg, state)
            if at == 0:
                q = out.pop(0)
            ks.append(out.pop(0))
            vs.append(out.pop(0))
            rs.append(out.pop(0))
            if at == 0:
                qa = out.pop(0)
            if at < span - 1:
                state = [qa, *out]
            else:
                o, qa = out
            if at == 0:
                state[1], b.x, b.y, c.shard, ext[2] = tie(state[1], b.x, b.y, c.shard, ext[2])
                b.forward()
                c.begin()
                while len(ext) < span:
                    ext.append(up(ext[-1]))
            if at == 1:
                state[1], b.xy, b.yx = tie(state[1], b.xy, b.yx)
                b.share()
            if at == span - 2:
                state[1], ext[-1], ups[0] = tie(state[1], ext[-1], ups[0])
                ups.append(up(ups[0]))
        o, c.x, c.y, d.shard, ups[1] = tie(o, c.x, c.y, d.shard, ups[1])
        ups.append(up(ups[1]))
        c.forward()
        d.begin()
        w_b = b.result()
        h1, h1_low, std1, r_mid, qc = mid("mid", scalars, o, x_low, 0, 6, True, *tables, w_b)
        qc, c.xy, c.yx, ups[2] = tie(qc, c.xy, c.yx, ups[2])
        c.share()
        while len(ups) < span:
            ups.append(up(ups[-1]))
        w_c = c.result()
        mems = [memory] + [ups[at] + downs[span - at] for at in range(1, span)]
        state, kcs, vcs, rcs, oc = None, [], [], [], None
        for at, slots in enumerate(halves):
            step = Step(f"cross_{at}", w_b, (3, 4), at, at == 0, at == 1, False)
            out = attend_step(step, scalars, [mems[i] for i in slots], tokens, mem_rows, *tables, free_aug, qc, free_seg, state)
            kcs.append(out.pop(0))
            vcs.append(out.pop(0))
            rcs.append(out.pop(0))
            if at == 0:
                state = out
                state[1], d.x, d.y = tie(state[1], d.x, d.y)
                d.forward()
            else:
                oc, qca = out
        oc, d.xy, d.yx = tie(oc, d.xy, d.yx)
        d.share()
        w_d = d.result()
        h2, h2_low, std2, r_co = mid("mid_cross", scalars, oc, h1, 1, 7, False, *tables, w_b)
        g, slope, r_fc1 = gelu_up(scalars, h2_low, fc1_down, fc1_up, w_c)
        y, d2, doc, gac, fc_grads = mlp(
            scalars, g, slope, h2, h2_low, std2, cotangent[0], r_fc1, r_co, oc,
            fc1_down, fc1_up, fc2_down, fc2_up, *tables, w_c, w_d, w_b,
        )
        g0, summed = everywhere(fc_grads)
        picks = g0[:, FC_ROWS["pick"], 0].astype(jnp.int32)

        state, dmem_parts, dqc, cross_grads, dmem = None, {}, None, None, None
        for at in (1, 0):
            step = Step(f"cross_back_{at}", w_b, (3, 4), at, at == 1, at == 0, False)
            out = back_step(step, scalars, qca, gac, qc, doc, kcs[at], vcs[at], free_aug, rcs[at], [mems[i] for i in halves[at]], mem_rows, *tables, state, None)
            if at:
                part, *state = out
                sent = list(halves[at])
            else:
                dmem, part, dqc, cross_grads = out
                sent = list(halves[at])[1:]
            for i, slot in enumerate(sent):
                dmem_parts[slot] = turn(part[i * mem_rows : (i + 1) * mem_rows], -slot)
        d1, do, ga, mid_grads = mid_back(scalars, dqc, d2, h1, h1_low, std1, r_mid, o, *tables, w_b)
        other, summed = tie(jnp.concatenate([mid_grads, cross_grads], axis=0), summed)
        g1, _ = everywhere(other)

        state, moving = None, None
        for at in reversed(range(span)):
            step = Step(f"self_back_{at}", w_a, (0, 1, 2) if at == 0 else (1, 2), at, at == span - 1, at == 0, True)
            out = back_step(step, scalars, qa, ga, q, do, ks[at], vs[at], augs[at], rs[at], [ext[at]], tokens, *tables, state, d1)
            if at == 0:
                dx, qkv_grads = out
                dx = dx + down(moving).astype(F32)
            else:
                part, *state = out
                moving = part if moving is None else (part.astype(F32) + down(moving).astype(F32)).astype(BF16)
        for part in dmem_parts.values():
            dmem = dmem + part.astype(F32)
        fcs = fc_total(picks, g0, (fc1_down.shape, fc1_up.shape, fc2_down.shape, fc2_up.shape))
        g2 = everywhere_now(qkv_grads)
        near = picks[own ^ jnp.array(order, jnp.int32)]
        projs = proj_total(jnp.concatenate([picks, near]), g0, g1, g2, proj_down.shape)
        return (y[None], dx[None], dmem[None], *projs, *fcs)

    return shards


def solution(mesh):
    count = mesh.shape["fsdp"]
    fine = Mesh(mesh.devices.reshape(count // 2, 2, mesh.shape["sp"]), ("chip", "core", "sp"))
    fsdp = ("chip", "core")
    row = P(fsdp, "sp", None)
    return jax.shard_map(
        make_shards(fine),
        mesh=fine,
        in_specs=(
            row,
            P(fsdp, "sp"),
            row,
            P(fsdp),
            P(None, None, fsdp, None),
            P(None, None, fsdp, None),
            P(None, fsdp, None),
            P(None, fsdp, None),
            P(),
            P(),
            P(),
            P(),
            P(),
            P(),
            row,
        ),
        out_specs=(row, row, row, P(), P(), P(), P(), P(), P()),
        check_vma=False,
    )
```

time: 744 us -> 574 us (0.77)
  the two profiles are of different devices: /device:TPU:0 before, /device:TPU:8 now
where the time goes in v2:
time: 574 us; the launch traced here: 564 us
  Pallas kernels  259 us (45%)
  waiting for transfers between devices  158 us (28%)
  starting transfers between devices  97.1 us (17%)
  other arithmetic  24 us (4%)
  between operations  15.5 us (3%)
  local copies, waits for them, and re-layouts  10.1 us (2%)
    pallas_call x6, Pallas kernels, back_step(): pl.pallas_call(functools.partial(back_step_kernel, step, len(xs)), grid_s...  90.2 us
    pallas_call x6, Pallas kernels, attend_step(): return list(call(scalars, *args, *step.w.arrays))  79.1 us
    ppermute x18, waiting for transfers between devices, across(): return lax.ppermute(values, 'chip', [(i, i ^ bit) for i in range(chips)])  47.3 us
    ppermute x6, waiting for transfers between devices, down(): return lax.ppermute(values, 'sp', [(i + 1, i) for i in range(span - 1)])  45.8 us
    pallas_call x1, Pallas kernels, mlp(): pl.pallas_call(functools.partial(mlp_kernel, w_up, w_down, w_mid), grid_s...  33.8 us
    ppermute x6, starting transfers between devices, up(): return lax.ppermute(values, 'sp', [(i, i + 1) for i in range(span - 1)])  29.7 us
    ppermute x3, waiting for transfers between devices, turn(): lax.ppermute(values, 'sp', [(i, (i + by) % span) for i in range(span)])  27.3 us
    ppermute x6, starting transfers between devices, down(): return lax.ppermute(values, 'sp', [(i + 1, i) for i in range(span - 1)])  21.5 us
  transfers between devices with their start and end apart: 60, of which 24 were waited for; matrix products, arithmetic and copies ran while one was open for 5% of the time, Pallas kernels for 38%

profile of v2, /device:TPU:8, one launch (start us, length us, event | category | flops | bytes accessed | tf_op | source)
XLA Modules:
  0.0 563.6 jit_solution(14024215847764672069)
XLA Ops:
  19.5 11.3 %collective-permute-done.4 = bf16[256,1024]{1,0:T(8,128)(2,1)S(1)} collective-permute-done((bf16[256,1024]{1,0:T(8,128)(2,1)S(1)}, bf16[256,1024]{1,0:T(8,128)(2,1)S(1)}, u32[]{:S(2)}, u32[]{:S(2)}) %collective-permute-start.4) | collective-permute-done | bytes 524320 | tf_op jit(solution)/shard_map/ppermute | solution.py:1010
  58.3 14.0 %self_0.1 = (bf16[384,1024]{1,0:T(8,128)(2,1)}, bf16[384,1024]{1,0:T(8,128)(2,1)}, bf16[384,1024]{1,0:T(8,128)(2,1)}, bf16[384,48]{1,0:T(8,128)(2,1)}, bf16[8,14...) custom-call(s32[3]{0:T(128)} %pad_add_fusion.sc_ref, bf16[400,1024]{1,0:T(8,128)(2,1)} %copy-done.12, ...), custom_call_target="tpu_custom_call" | custom-call | flops 3019898880 | bytes 7864320 | tf_op jit(solution)/shard_map/self_0/pallas_call | solution.py:384
  96.4 15.6 %self_1.1 = (bf16[384,1024]{1,0:T(8,128)(2,1)}, bf16[384,1024]{1,0:T(8,128)(2,1)}, bf16[384,48]{1,0:T(8,128)(2,1)}, f32[8,144,768]{2,1,0:T(8,128)}, f32[8,8,768]{2,1,0:T(8,128)}) custom-call(s32[3]{0:T(128)} %pad_add_fusion.sc_ref, bf16[400,1024]{1,0:T(8,128)(2,1)} %collective-permute-done.1.refs_0_.refs_10_, bf16[1,8,8,16,1024]{4,3,2,1,0:T(8,128)(2,1)} %refs_8_.11, ...), custom_call_target="tpu_custom_call" | custom-call | flops 2214592512 | bytes 7864320 | tf_op jit(solution)/shard_map/self_1/pallas_call | solution.py:384
  114.1 8.6 %self_2.1 = (bf16[384,1024]{1,0:T(8,128)(2,1)}, bf16[384,1024]{1,0:T(8,128)(2,1)}, bf16[384,48]{1,0:T(8,128)(2,1)}, f32[8,144,768]{2,1,0:T(8,128)}, f32[8,8,768]{2,1,0:T(8,128)}) custom-call(s32[3]{0:T(128)} %pad_add_fusion.sc_ref, bf16[400,1024]{1,0:T(8,128)(2,1)} %collective-permute-done.14.refs_0_.refs_10_, bf16[1,8,8,16,1024]{4,3,2,1,0:T(8,128)(2,1)} %refs_8_.11, ...), custom_call_target="tpu_custom_call" | custom-call | flops 2214592512 | bytes 7864320 | tf_op jit(solution)/shard_map/self_2/pallas_call | solution.py:384
  122.7 10.2 %collective-permute-start.20 = (bf16[256,1024]{1,0:T(8,128)(2,1)S(1)}, bf16[256,1024]{1,0:T(8,128)(2,1)}, u32[]{:S(2)}, u32[]{:S(2)}) collective-permute-start(bf16[256,1024]{1,0:T(8,128)(2,1)S(1)} %bitcast.39), channel_id=1, source_target_pairs={{0,1},{1,2},{2,3},{4,5},{5,6},{6,7},{8,9},{9,10},{10,11},{12,13},{... | collective-permute-start | bytes 1572872 | tf_op jit(solution)/shard_map/ppermute | solution.py:1007
  134.5 9.5 %collective-permute-done.20 = bf16[256,1024]{1,0:T(8,128)(2,1)} collective-permute-done((bf16[256,1024]{1,0:T(8,128)(2,1)S(1)}, bf16[256,1024]{1,0:T(8,128)(2,1)}, u32[]{:S(2)}, u32[]{:S(2)}) %collective-permute-start.20) | collective-permute-done | bytes 524320 | tf_op jit(solution)/shard_map/ppermute | solution.py:1007
  172.3 8.2 %mid.1 = (f32[384,1024]{1,0:T(8,128)}, bf16[384,1024]{1,0:T(8,128)(2,1)}, f32[384,1]{1,0:T(8,128)}, bf16[384,32]{1,0:T(8,128)(2,1)}, bf16[384,1024]{1,0:T(8,128)(2,1)}) custom-call(s32[3]{0:T(128)} %pad_add_fusion.sc_ref, bf16[384,1024]{1,0:T(8,128)(2,1)} %get-tuple-element.146.o_ref, bf16[384,1024]{1,0:T(8,128)(2,1)} %bitcast.34, ...), custom_call_target="tpu_custom_call" | custom-call | flops 1610612736 | bytes 8912896 | tf_op jit(solution)/shard_map/mid/pallas_call | solution.py:623
  189.8 15.7 %cross_0.1 = (bf16[512,1024]{1,0:T(8,128)(2,1)}, bf16[512,1024]{1,0:T(8,128)(2,1)}, bf16[512,32]{1,0:T(8,128)(2,1)}, bf16[8,144,768]{2,1,0:T(8,128)(2,1)}, f32[8,144,768]{2,1,0:T(8,128)}, /*index=5*/f32[8,8,768]{2,1,0:T(8,128)}) custom-call(s32[3]{0:T(128)} %pad_add_fusion.sc_ref, bf16[256,1024]{1,0:T(8,128)(2,1)} %bitcast.36, ...), custom_call_target="tpu_custom_call" | custom-call | flops 2952790016 | bytes 7864320 | tf_op jit(solution)/shard_map/cross_0/pallas_call | solution.py:384
  210.3 10.5 %collective-permute-done.33.refs_16_ = bf16[256,1024]{1,0:T(8,128)(2,1)S(1)} collective-permute-done((bf16[256,1024]{1,0:T(8,128)(2,1)S(1)}, bf16[256,1024]{1,0:T(8,128)(2,1)S(1)}, u32[]{:S(2)}, u32[]{:S(2)}) %collective-permute-start.33) | collective-permute-done | bytes 524320 | tf_op jit(solution)/shard_map/ppermute | solution.py:1019
  227.1 17.3 %cross_1.1 = (bf16[512,1024]{1,0:T(8,128)(2,1)}, bf16[512,1024]{1,0:T(8,128)(2,1)}, bf16[512,32]{1,0:T(8,128)(2,1)}, bf16[384,1024]{1,0:T(8,128)(2,1)}, bf16[8,144,768]{2,1,0:T(8,128)(2,1)}) custom-call(s32[3]{0:T(128)} %pad_add_fusion.sc_ref, bf16[256,1024]{1,0:T(8,128)(2,1)} %add.58.refs_0_.refs_10_, bf16[256,1024]{1,0:T(8,128)(2,1)} %add.59.refs_1_.refs_11_, ...), custom_call_target="tpu_custom_call" | custom-call | flops 2952790016 | bytes 7864320 | tf_op jit(solution)/shard_map/cross_1/pallas_call | solution.py:384
  252.5 15.2 %gelu_up.1 = (bf16[384,4096]{1,0:T(8,128)(2,1)}, bf16[384,4096]{1,0:T(8,128)(2,1)}, bf16[384,16]{1,0:T(8,128)(2,1)}) custom-call(s32[3]{0:T(128)} %pad_add_fusion.sc_ref, bf16[384,1024]{1,0:T(8,128)(2,1)} %get-tuple-element.166.x_ref.h2_low_ref, bf16[1,8,16,1024]{3,2,1,0:T(8,128)(2,1)} %a1_ref.1, bf16[1,8,16,4096]{3,2,1,0:T(8,128)(2,1)} %b1_ref.1, ...), custom_call_target="tpu_custom_call" | custom-call | flops 3221225472 | bytes 14680064 | tf_op jit(solution)/shard_map/gelu_up/pallas_call | solution.py:660
  268.5 33.8 %mlp.1 = (bf16[384,1024]{1,0:T(8,128)(2,1)}, f32[384,1024]{1,0:T(8,128)}, bf16[384,1024]{1,0:T(8,128)(2,1)}, bf16[8,144,768]{2,1,0:T(8,128)(2,1)}, bf16[208,1024]{1,0:T(8,128)(2,1)}) custom-call(s32[3]{0:T(128)} %pad_add_fusion.sc_ref, bf16[384,4096]{1,0:T(8,128)(2,1)} %get-tuple-element.169.g_ref, bf16[384,4096]{1,0:T(8,128)(2,1)} %get-tuple-element.170.slope_ref, ...), custom_call_target="tpu_custom_call" | custom-call | flops 9663676416 | bytes 23068672 | tf_op jit(solution)/shard_map/mlp/pallas_call | solution.py:771
  302.4 18.6 %cross_back_1.1 = (bf16[512,1024]{1,0:T(8,128)(2,1)}, f32[8,128,384]{2,1,0:T(8,128)}, f32[64,1024]{1,0:T(8,128)}) custom-call(s32[3]{0:T(128)} %pad_add_fusion.sc_ref, bf16[8,144,768]{2,1,0:T(8,128)(2,1)} %get-tuple-element.179.refs_0_, bf16[8,144,768]{2,1,0:T(8,128)(2,1)} %get-tuple-element.180.refs_1_, ...), custom_call_target="tpu_custom_call" | custom-call | flops 4160749568 | bytes 9437184 | tf_op jit(solution)/shard_map/cross_back_1/pallas_call | solution.py:550
  321.0 19.2 %cross_back_0.1 = (f32[256,1024]{1,0:T(8,128)}, bf16[256,1024]{1,0:T(8,128)(2,1)}, bf16[384,1024]{1,0:T(8,128)(2,1)}, bf16[64,1024]{1,0:T(8,128)(2,1)}) custom-call(s32[3]{0:T(128)} %pad_add_fusion.sc_ref, bf16[8,144,768]{2,1,0:T(8,128)(2,1)} %get-tuple-element.179.refs_0_, bf16[8,144,768]{2,1,0:T(8,128)(2,1)} %get-tuple-element.180.refs_1_, ...), custom_call_target="tpu_custom_call" | custom-call | flops 4160749568 | bytes 9437184 | tf_op jit(solution)/shard_map/cross_back_0/pallas_call | solution.py:550
  340.1 11.0 %mid_back.1 = (f32[384,1024]{1,0:T(8,128)}, bf16[384,1024]{1,0:T(8,128)(2,1)}, bf16[8,144,768]{2,1,0:T(8,128)(2,1)}, bf16[64,1024]{1,0:T(8,128)(2,1)}) custom-call(s32[3]{0:T(128)} %pad_add_fusion.sc_ref, bf16[384,1024]{1,0:T(8,128)(2,1)} %get-tuple-element.190.dqc_ref, f32[384,1024]{1,0:T(8,128)} %get-tuple-element.191.d2_ref, ...), custom_call_target="tpu_custom_call" | custom-call | flops 1610612736 | bytes 12058624 | tf_op jit(solution)/shard_map/mid_back/pallas_call | solution.py:857
  353.6 8.6 %self_back_3.1 = (bf16[384,1024]{1,0:T(8,128)(2,1)}, f32[8,128,384]{2,1,0:T(8,128)}, f32[64,1024]{1,0:T(8,128)}) custom-call(s32[3]{0:T(128)} %pad_add_fusion.sc_ref, bf16[8,144,768]{2,1,0:T(8,128)(2,1)} %get-tuple-element.178.refs_0_, bf16[8,144,768]{2,1,0:T(8,128)(2,1)} %get-tuple-element.195.refs_1_, bf16[384,1024]{1,0:T(8,128)(2,1)} %get-tuple-element.196.refs_2_, ...), custom_call_target="tpu_custom_call" | custom-call | flops 3120562176 | bytes 9437184 | tf_op jit(solution)/shard_map/self_back_3/pallas_call | solution.py:550
  362.2 8.6 %self_back_2.1 = (bf16[384,1024]{1,0:T(8,128)(2,1)}, f32[8,128,384]{2,1,0:T(8,128)}, f32[64,1024]{1,0:T(8,128)}) custom-call(s32[3]{0:T(128)} %pad_add_fusion.sc_ref, bf16[8,144,768]{2,1,0:T(8,128)(2,1)} %get-tuple-element.178.refs_0_, bf16[8,144,768]{2,1,0:T(8,128)(2,1)} %get-tuple-element.195.refs_1_, bf16[384,1024]{1,0:T(8,128)(2,1)} %get-tuple-element.196.refs_2_, ...), custom_call_target="tpu_custom_call" | custom-call | flops 3120562176 | bytes 9437184 | tf_op jit(solution)/shard_map/self_back_2/pallas_call | solution.py:550
  370.8 16.1 %self_back_1.1 = (bf16[384,1024]{1,0:T(8,128)(2,1)}, f32[8,128,384]{2,1,0:T(8,128)}, f32[64,1024]{1,0:T(8,128)}) custom-call(s32[3]{0:T(128)} %pad_add_fusion.sc_ref, bf16[8,144,768]{2,1,0:T(8,128)(2,1)} %get-tuple-element.178.refs_0_, bf16[8,144,768]{2,1,0:T(8,128)(2,1)} %get-tuple-element.195.refs_1_, bf16[384,1024]{1,0:T(8,128)(2,1)} %get-tuple-element.196.refs_2_, ...), custom_call_target="tpu_custom_call" | custom-call | flops 3120562176 | bytes 9437184 | tf_op jit(solution)/shard_map/self_back_1/pallas_call | solution.py:550
  393.1 19.2 %self_back_0.1 = (f32[384,1024]{1,0:T(8,128)}, bf16[96,1024]{1,0:T(8,128)(2,1)}) custom-call(s32[3]{0:T(128)} %pad_add_fusion.sc_ref, bf16[8,144,768]{2,1,0:T(8,128)(2,1)} %get-tuple-element.178.refs_0_, bf16[8,144,768]{2,1,0:T(8,128)(2,1)} %get-tuple-element.195.refs_1_, bf16[384,1024]{1,0:T(8,128)(2,1)} %get-tuple-element.196.refs_2_, ...), custom_call_target="tpu_custom_call" | custom-call | flops 3120562176 | bytes 9437184 | tf_op jit(solution)/shard_map/self_back_0/pallas_call | solution.py:550
  419.3 16.3 %collective-permute-start.52 = (bf16[96,1024]{1,0:T(8,128)(2,1)S(1)}, bf16[96,1024]{1,0:T(8,128)(2,1)S(1)}, u32[]{:S(2)}, u32[]{:S(2)}) collective-permute-start(bf16[96,1024]{1,0:T(8,128)(2,1)S(1)} %add_convert_fusion.3), channel_id=1, source_target_pairs={{0,2},{1,3},{2,0},{3,1},{4,6},{5,7},{6,4},{7,5},{8,10},{9,11},{10,... | collective-permute-start | bytes 589832 | tf_op jit(solution)/shard_map/ppermute | solution.py:1016
  435.5 18.4 %collective-permute-done.52 = bf16[96,1024]{1,0:T(8,128)(2,1)S(1)} collective-permute-done((bf16[96,1024]{1,0:T(8,128)(2,1)S(1)}, bf16[96,1024]{1,0:T(8,128)(2,1)S(1)}, u32[]{:S(2)}, u32[]{:S(2)}) %collective-permute-start.52) | collective-permute-done | bytes 196640 | tf_op jit(solution)/shard_map/ppermute | solution.py:1016
  483.8 27.3 %collective-permute-done.50 = bf16[256,1024]{1,0:T(8,128)(2,1)S(1)} collective-permute-done((bf16[256,1024]{1,0:T(8,128)(2,1)S(1)}, bf16[256,1024]{1,0:T(8,128)(2,1)S(1)}, u32[]{:S(2)}, u32[]{:S(2)}) %collective-permute-start.50) | collective-permute-done | bytes 524320 | tf_op jit(solution)/shard_map/ppermute | solution.py:1013
  513.7 24.7 %collective-permute-done.47 = bf16[384,1024]{1,0:T(8,128)(2,1)S(1)} collective-permute-done((bf16[384,1024]{1,0:T(8,128)(2,1)S(1)}, bf16[384,1024]{1,0:T(8,128)(2,1)S(1)}, u32[]{:S(2)}, u32[]{:S(2)}) %collective-permute-start.47) | collective-permute-done | bytes 786464 | tf_op jit(solution)/shard_map/ppermute | solution.py:1010
  548.3 8.6 %proj_total.1 = (f32[1,8,8,16,1024]{4,3,2,1,0:T(8,128)}, f32[1,8,8,16,1024]{4,3,2,1,0:T(8,128)}) custom-call(s32[16]{0:T(128)} %pad_add_fusion.1.picks_ref, bf16[8,208,1024]{2,1,0:T(8,128)(2,1)} %bitcast.32, bf16[8,128,1024]{2,1,0:T(8,128)(2,1)} %all-gather.4.cloned.1.call-done.g1_ref, bf16[8,96,1024]{2,1,0:T(8,128)(2,1)} %pad_maximum_fusion.g2_ref), custom_call_target="tpu_custom_call" | custom-call | bytes 12582912 | tf_op jit(solution)/shard_map/proj_total/pallas_call | solution.py:943
  (239 shorter events, 181.9 us)
Async XLA Ops:
  7.2 345.6 %all-reduce.4.cloned.1.call-start = ((), (), s32[]{:S(2)}) async-start(), calls=%async_computation | async-start | bytes 851968 | tf_op jit(solution)/shard_map/psum | solution.py:1030
  77.8 44.8 %collective-permute-start.18 = (bf16[128,4096]{1,0:T(8,128)(2,1)}, bf16[128,4096]{1,0:T(8,128)(2,1)}, u32[]{:S(2)}, u32[]{:S(2)}) collective-permute-start(bf16[128,4096]{1,0:T(8,128)(2,1)} %bitcast.7.refs_0_), channel_id=1, source_target_pairs={{0,8},{8,0},{16,24},{24,16},{1,9},{9,1},{17,25},{25,17},{2,10},{10... | collective-permute-start | bytes 3145736 | tf_op jit(solution)/shard_map/ppermute | solution.py:1019
  78.7 34.9 %collective-permute-start.17 = (bf16[400,1024]{1,0:T(8,128)(2,1)}, bf16[400,1024]{1,0:T(8,128)(2,1)}, u32[]{:S(2)}, u32[]{:S(2)}) collective-permute-start(bf16[400,1024]{1,0:T(8,128)(2,1)} %collective-permute-done.14.refs_0_.refs_10_), channel_id=1, source_target_pairs={{0,1},{1,2},{2,3},{4,5},{5,6},{6,7},{8,9},{9,10},{10,11},{12,13},{... | collective-permute-start | bytes 2457608 | tf_op jit(solution)/shard_map/ppermute | solution.py:1007
  82.1 50.8 %collective-permute-start.19 = (bf16[128,4096]{1,0:T(8,128)(2,1)}, bf16[128,4096]{1,0:T(8,128)(2,1)}, u32[]{:S(2)}, u32[]{:S(2)}) collective-permute-start(bf16[128,4096]{1,0:T(8,128)(2,1)} %bitcast.7.refs_0_), channel_id=1, source_target_pairs={{0,16},{8,24},{16,0},{24,8},{1,17},{9,25},{17,1},{25,9},{2,18},{10... | collective-permute-start | bytes 3145736 | tf_op jit(solution)/shard_map/ppermute | solution.py:1019
  95.5 58.5 %collective-permute-start.21 = (bf16[640,1024]{1,0:T(8,128)(2,1)S(1)}, bf16[640,1024]{1,0:T(8,128)(2,1)}, u32[]{:S(2)}, u32[]{:S(2)}) collective-permute-start(bf16[640,1024]{1,0:T(8,128)(2,1)S(1)} %pad_maximum_fusion.1.refs_0_.refs_7_.refs_8_.refs_20_.refs_12_.refs_14_), channel_id=1, source_target_pairs={{0,4},{4,0},{1,5},{5,1},{2,6},{6,2},{3,7},{7,3},{8,12},{12,8},{9,1... | collective-permute-start | bytes 3932168 | tf_op jit(solution)/shard_map/ppermute | solution.py:1022
  113.5 44.1 %collective-permute-start.22 = (bf16[640,1024]{1,0:T(8,128)(2,1)S(1)}, bf16[640,1024]{1,0:T(8,128)(2,1)}, u32[]{:S(2)}, u32[]{:S(2)}) collective-permute-start(bf16[640,1024]{1,0:T(8,128)(2,1)S(1)} %collective-permute-done.12.refs_2_.refs_9_.refs_10_.refs_22_.refs_14_.refs_16_), channel_id=1, source_target_pairs={{0,4},{4,0},{1,5},{5,1},{2,6},{6,2},{3,7},{7,3},{8,12},{12,8},{9,1... | collective-permute-start | bytes 3932168 | tf_op jit(solution)/shard_map/ppermute | solution.py:1022
  113.6 44.6 %collective-permute-start.23 = (bf16[640,1024]{1,0:T(8,128)(2,1)}, bf16[640,1024]{1,0:T(8,128)(2,1)}, u32[]{:S(2)}, u32[]{:S(2)}) collective-permute-start(bf16[640,1024]{1,0:T(8,128)(2,1)} %collective-permute-done.13.refs_4_.refs_11_.refs_12_.refs_24_.refs_16_.refs_18_), channel_id=1, source_target_pairs={{0,4},{4,0},{1,5},{5,1},{2,6},{6,2},{3,7},{7,3},{8,12},{12,8},{9,1... | collective-permute-start | bytes 3932168 | tf_op jit(solution)/shard_map/ppermute | solution.py:1022
  156.7 48.9 %collective-permute-start.31 = (bf16[512,1024]{1,0:T(8,128)(2,1)}, bf16[512,1024]{1,0:T(8,128)(2,1)S(1)}, u32[]{:S(2)}, u32[]{:S(2)}) collective-permute-start(bf16[512,1024]{1,0:T(8,128)(2,1)} %bitcast.8.refs_10_), channel_id=1, source_target_pairs={{0,8},{8,0},{16,24},{24,16},{1,9},{9,1},{17,25},{25,17},{2,10},{10... | collective-permute-start | bytes 3145736 | tf_op jit(solution)/shard_map/ppermute | solution.py:1019
  157.7 48.5 %collective-permute-start.32 = (bf16[512,1024]{1,0:T(8,128)(2,1)}, bf16[512,1024]{1,0:T(8,128)(2,1)S(1)}, u32[]{:S(2)}, u32[]{:S(2)}) collective-permute-start(bf16[512,1024]{1,0:T(8,128)(2,1)} %bitcast.8.refs_10_), channel_id=1, source_target_pairs={{0,16},{8,24},{16,0},{24,8},{1,17},{9,25},{17,1},{25,9},{2,18},{10... | collective-permute-start | bytes 3145736 | tf_op jit(solution)/shard_map/ppermute | solution.py:1019
  169.0 37.4 %collective-permute-start.35 = (bf16[128,4096]{1,0:T(8,128)(2,1)}, bf16[128,4096]{1,0:T(8,128)(2,1)S(1)}, u32[]{:S(2)}, u32[]{:S(2)}) collective-permute-start(bf16[128,4096]{1,0:T(8,128)(2,1)} %bitcast.7.refs_0_), channel_id=1, source_target_pairs={{0,4},{4,0},{1,5},{5,1},{2,6},{6,2},{3,7},{7,3},{8,12},{12,8},{9,1... | collective-permute-start | bytes 3145736 | tf_op jit(solution)/shard_map/ppermute | solution.py:1022
  205.6 38.8 %collective-permute-start.36 = (bf16[128,4096]{1,0:T(8,128)(2,1)}, bf16[128,4096]{1,0:T(8,128)(2,1)}, u32[]{:S(2)}, u32[]{:S(2)}) collective-permute-start(bf16[128,4096]{1,0:T(8,128)(2,1)} %collective-permute-done.18.refs_2_), channel_id=1, source_target_pairs={{0,4},{4,0},{1,5},{5,1},{2,6},{6,2},{3,7},{7,3},{8,12},{12,8},{9,1... | collective-permute-start | bytes 3145736 | tf_op jit(solution)/shard_map/ppermute | solution.py:1022
  206.2 38.8 %collective-permute-start.37 = (bf16[128,4096]{1,0:T(8,128)(2,1)}, bf16[128,4096]{1,0:T(8,128)(2,1)}, u32[]{:S(2)}, u32[]{:S(2)}) collective-permute-start(bf16[128,4096]{1,0:T(8,128)(2,1)} %collective-permute-done.19.refs_4_), channel_id=1, source_target_pairs={{0,4},{4,0},{1,5},{5,1},{2,6},{6,2},{3,7},{7,3},{8,12},{12,8},{9,1... | collective-permute-start | bytes 3145736 | tf_op jit(solution)/shard_map/ppermute | solution.py:1022
  209.9 57.7 %collective-permute-start.40 = (bf16[512,1024]{1,0:T(8,128)(2,1)}, bf16[512,1024]{1,0:T(8,128)(2,1)}, u32[]{:S(2)}, u32[]{:S(2)}) collective-permute-start(bf16[512,1024]{1,0:T(8,128)(2,1)} %bitcast.8.refs_10_), channel_id=1, source_target_pairs={{0,4},{4,0},{1,5},{5,1},{2,6},{6,2},{3,7},{7,3},{8,12},{12,8},{9,1... | collective-permute-start | bytes 3145736 | tf_op jit(solution)/shard_map/ppermute | solution.py:1022
  220.8 46.9 %collective-permute-start.41 = (bf16[512,1024]{1,0:T(8,128)(2,1)S(1)}, bf16[512,1024]{1,0:T(8,128)(2,1)}, u32[]{:S(2)}, u32[]{:S(2)}) collective-permute-start(bf16[512,1024]{1,0:T(8,128)(2,1)S(1)} %collective-permute-done.31.refs_12_), channel_id=1, source_target_pairs={{0,4},{4,0},{1,5},{5,1},{2,6},{6,2},{3,7},{7,3},{8,12},{12,8},{9,1... | collective-permute-start | bytes 3145736 | tf_op jit(solution)/shard_map/ppermute | solution.py:1022
  222.9 44.9 %collective-permute-start.42 = (bf16[512,1024]{1,0:T(8,128)(2,1)S(1)}, bf16[512,1024]{1,0:T(8,128)(2,1)}, u32[]{:S(2)}, u32[]{:S(2)}) collective-permute-start(bf16[512,1024]{1,0:T(8,128)(2,1)S(1)} %collective-permute-done.32.refs_14_), channel_id=1, source_target_pairs={{0,4},{4,0},{1,5},{5,1},{2,6},{6,2},{3,7},{7,3},{8,12},{12,8},{9,1... | collective-permute-start | bytes 3145736 | tf_op jit(solution)/shard_map/ppermute | solution.py:1022
  302.3 90.8 %all-reduce.6.cloned.1.call-start = ((), (), s32[]{:S(2)}) async-start(), calls=%async_computation.1 | async-start | bytes 524288 | tf_op jit(solution)/shard_map/psum | solution.py:1030
  352.8 187.0 %all-gather.6.cloned.1.call-start = ((), (), s32[]{:S(2)}) async-start(), calls=%async_computation.3 | async-start | bytes 3833856 | tf_op jit(solution)/shard_map/all_gather | solution.py:1031
  353.5 194.8 %all-gather.4.cloned.1.call-start = ((), (), s32[]{:S(2)}) async-start(), calls=%async_computation.2 | async-start | bytes 2359296 | tf_op jit(solution)/shard_map/all_gather | solution.py:1031
  413.0 42.4 %collective-permute-start.45 = (bf16[384,1024]{1,0:T(8,128)(2,1)S(1)}, bf16[384,1024]{1,0:T(8,128)(2,1)S(1)}, u32[]{:S(2)}, u32[]{:S(2)}) collective-permute-start(bf16[384,1024]{1,0:T(8,128)(2,1)S(1)} %copy-done.35), channel_id=1, source_target_pairs={{1,0},{2,1},{3,2},{5,4},{6,5},{7,6},{9,8},{10,9},{11,10},{13,12},{... | collective-permute-start | bytes 2359304 | tf_op jit(solution)/shard_map/ppermute | solution.py:1010
  462.2 48.8 %collective-permute-start.50 = (bf16[256,1024]{1,0:T(8,128)(2,1)S(1)}, bf16[256,1024]{1,0:T(8,128)(2,1)S(1)}, u32[]{:S(2)}, u32[]{:S(2)}) collective-permute-start(bf16[256,1024]{1,0:T(8,128)(2,1)S(1)} %copy-done.36), channel_id=1, source_target_pairs={{0,3},{1,0},{2,1},{3,2},{4,7},{5,4},{6,5},{7,6},{8,11},{9,8},{10,9... | collective-permute-start | bytes 1572872 | tf_op jit(solution)/shard_map/ppermute | solution.py:1013
  465.1 46.0 %collective-permute-start.48 = (bf16[256,1024]{1,0:T(8,128)(2,1)S(1)}, bf16[256,1024]{1,0:T(8,128)(2,1)S(1)}, u32[]{:S(2)}, u32[]{:S(2)}) collective-permute-start(bf16[256,1024]{1,0:T(8,128)(2,1)S(1)} %get-tuple-element.239), channel_id=1, source_target_pairs={{0,2},{1,3},{2,0},{3,1},{4,6},{5,7},{6,4},{7,5},{8,10},{9,11},{10,... | collective-permute-start | bytes 1572872 | tf_op jit(solution)/shard_map/ppermute | solution.py:1013
  465.2 45.9 %collective-permute-start.49 = (bf16[256,1024]{1,0:T(8,128)(2,1)S(1)}, bf16[256,1024]{1,0:T(8,128)(2,1)S(1)}, u32[]{:S(2)}, u32[]{:S(2)}) collective-permute-start(bf16[256,1024]{1,0:T(8,128)(2,1)S(1)} %get-tuple-element.240), channel_id=1, source_target_pairs={{0,1},{1,2},{2,3},{3,0},{4,5},{5,6},{6,7},{7,4},{8,9},{9,10},{10,1... | collective-permute-start | bytes 1572872 | tf_op jit(solution)/shard_map/ppermute | solution.py:1013
  471.2 41.1 %collective-permute-start.55 = (bf16[4,96,1024]{2,1,0:T(8,128)(2,1)S(1)}, bf16[4,96,1024]{2,1,0:T(8,128)(2,1)S(1)}, u32[]{:S(2)}, u32[]{:S(2)}) collective-permute-start(bf16[4,96,1024]{2,1,0:T(8,128)(2,1)S(1)} %pad_maximum_fusion.2), channel_id=1, source_target_pairs={{0,4},{4,0},{1,5},{5,1},{2,6},{6,2},{3,7},{7,3},{8,12},{12,8},{9,1... | collective-permute-start | bytes 2359304 | tf_op jit(solution)/shard_map/ppermute | solution.py:1022
  479.3 59.1 %collective-permute-start.47 = (bf16[384,1024]{1,0:T(8,128)(2,1)S(1)}, bf16[384,1024]{1,0:T(8,128)(2,1)S(1)}, u32[]{:S(2)}, u32[]{:S(2)}) collective-permute-start(bf16[384,1024]{1,0:T(8,128)(2,1)S(1)} %add_convert_fusion), channel_id=1, source_target_pairs={{1,0},{2,1},{3,2},{5,4},{6,5},{7,6},{9,8},{10,9},{11,10},{13,12},{... | collective-permute-start | bytes 2359304 | tf_op jit(solution)/shard_map/ppermute | solution.py:1010
  (74 other events, 1238.5 us)
Sparse Core Ops, SparseCore 0:
  302.4 41.8 all-reduce.3
  352.9 40.0 all-reduce.5
  394.9 33.1 all-gather.5
  429.9 27.8 all-gather.3
